TPU v7x, 512 devices: a whole 4x8x8 slice. The times are simulated.
512 devices in a mesh: dp: 16 (over z, y_lo), tensor: 32 (over x, y_hi, core).
Axes of the slice: x: 4, y: 8 (y_hi: 4, y_lo: 2; y = y_hi * 2 + y_lo), z: 8, core: 2. Of those that a mesh axis runs over, the one named last changes fastest.
Arguments:
- activations: bfloat16 [2048, 8192], P('tensor', 'dp'), may hold values from -6 to 6
- grad_out: bfloat16 [2048, 28672], P('dp', 'tensor'), may hold values from -6 to 6
- weight: bfloat16 [8192, 28672], P('dp', 'tensor'), may hold values from -0.0625 to 0.0625
- block_mask: int32 [64, 224], P('dp', 'tensor'), may hold values from 0 to 1, as said below
Outputs:
- grad_input: bfloat16 [2048, 8192], P('tensor', 'dp')
- grad_weight: bfloat16 [8192, 28672], P('dp', 'tensor')
Inputs may be any that keep to these rules, and one draw needn't show every extreme that they name: `block_mask`: each entry is 0 or 1; the share of ones differs from one column of blocks to the next and is a quarter on average.
All inputs are finite; a program needn't handle non-finite values.
Results may differ from a plain program's by a relative error of at most 0.019.
Values may be sent and summed in bfloat16 or wider, within the bound.
No kernel may reach another device: no remote copies, remote signals or barrier semaphores. Data moves between devices by JAX's collectives and lax.ppermute only.
A program may use at most 64 MiB of HBM per device.

v0:
```python
import math

import jax
import jax.numpy as jnp
from jax import lax
from jax.sharding import PartitionSpec as P


def expand_mask(block_mask, side):
    rows, cols = block_mask.shape
    flags = block_mask.astype(jnp.bfloat16)
    spread = jnp.broadcast_to(flags[:, None, :, None], (rows, side, cols, side))
    return spread.reshape(rows * side, cols * side)


def shards(activations, grad_out, weight, block_mask):
    side = weight.shape[0] // block_mask.shape[0]
    keep_mask = expand_mask(block_mask, side)
    masked = weight * keep_mask
    whole_input = lax.all_gather(activations, "tensor", axis=0, tiled=True)
    tokens = whole_input.shape[0]
    factor = 1.0 / math.sqrt(tokens)
    partial_value = lax.dot_general(
        lax.all_gather(grad_out, "dp", axis=0, tiled=True),
        masked,
        (((1,), (1,)), ((), ())),
        preferred_element_type=jnp.float32,
    )
    weight_sum = lax.dot_general(
        whole_input,
        lax.all_gather(grad_out, "dp", axis=0, tiled=True),
        (((0,), (0,)), ((), ())),
        preferred_element_type=jnp.float32,
    )
    grad_weight = (weight_sum * keep_mask.astype(jnp.float32) * factor).astype(jnp.bfloat16)
    grad_input = lax.psum_scatter(
        partial_value.astype(jnp.bfloat16), "tensor", scatter_dimension=0, tiled=True
    )
    return (grad_input, grad_weight)


def solution(mesh):
    placed = (P("tensor", "dp"), P("dp", "tensor"), P("dp", "tensor"), P("dp", "tensor"))
    return jax.shard_map(
        shards,
        mesh=mesh,
        in_specs=placed,
        out_specs=(P("tensor", "dp"), P("dp", "tensor")),
        check_vma=False,
    )
```

profile of v0, /device:TPU:6, one launch (start us, length us, event | category | flops | bytes accessed | tf_op | source)
XLA Modules:
  0.0 276.6 jit_solution(16828556911687920237)
XLA Ops:
  7.2 0.0 all-gather.3.cloned.1.call-start
  7.2 0.7 all-gather.3.cloned.1.call-update
  7.9 0.0 all-gather.5.cloned.1.call-start
  7.9 0.7 all-gather.5.cloned.1.call-update
  8.6 0.0 reduce-scatter.4.cloned.1.call-start
  8.7 0.7 convert_element_type.15
  9.4 0.1 copy.11
  9.5 2.2 copy.12
  11.7 96.5 %all-gather.3.cloned.1.call-done = bf16[2048,896]{1,0:T(8,128)(2,1)} async-done(((bf16[128,896]{1,0:T(8,128)(2,1)}), bf16[2048,896]{1,0:T(8,128)(2,1)}) %all-gather.3.cloned.1.call-update) | async-done | bytes 3670032 | tf_op jit(solution)/shard_map/all_gather | solution.py:24
  108.2 0.3 broadcast_in_dim.2
  108.5 4.7 %fusion = bf16[2048,512]{0,1:T(8,128)(2,1)S(1)} fusion(bf16[2048,896]{1,0:T(8,128)(2,1)} %all-gather.3.cloned.1.call-done, bf16[512,896]{0,1:T(8,128)(2,1)} %copy.12, bf16[112,8,4,128]{3,2,1,0:T(4,128)(2,1)S(1)} %bitcast.16), kind=kOutput, calls=%fused_computation.1 | convolution fusion | flops 1880555520 | bytes 7602176 | tf_op jit(solution)/shard_map/dot_general | solution.py:23
  113.2 2.5 copy.15
  115.7 0.0 reduce-scatter.4.cloned.1.call-update
  115.8 0.2 copy.22
  115.9 0.6 copy.13
  116.5 50.6 %all-gather.5.cloned.1.call-done = bf16[2048,512]{1,0:T(8,128)(2,1)} async-done(((bf16[64,512]{1,0:T(8,128)(2,1)}), bf16[2048,512]{1,0:T(8,128)(2,1)}) %all-gather.5.cloned.1.call-update) | async-done | bytes 2097168 | tf_op jit(solution)/shard_map/all_gather | solution.py:20
  167.2 5.9 %multiply_convert_fusion = bf16[512,896]{1,0:T(8,128)(2,1)} fusion(bf16[512,896]{1,0:T(8,128)(2,1)S(1)} %copy.13, bf16[2048,512]{1,0:T(8,128)(2,1)} %all-gather.5.cloned.1.call-done, bf16[2048,896]{1,0:T(8,128)(2,1)} %all-gather.3.cloned.1.call-done), kind=kOutput, calls=%fused_computation.2 | convolution fusion | flops 1880883200 | bytes 7602176 | tf_op jit(solution)/shard_map/dot_general | solution.py:29
  173.1 96.9 %reduce-scatter.4.cloned.1.call-done = bf16[64,512]{1,0:T(8,128)(2,1)} async-done(((bf16[2048,512]{1,0:T(8,128)(2,1)}), bf16[64,512]{1,0:T(8,128)(2,1)}) %reduce-scatter.4.cloned.1.call-update) | async-done | bytes 65552
Async XLA Ops:
  7.2 101.1 %all-gather.3.cloned.1.call-start = ((), (), s32[]{:S(2)}) async-start(), calls=%async_computation.1 | async-start | bytes 3899392 | tf_op jit(solution)/shard_map/all_gather | solution.py:24
  7.9 159.3 %all-gather.5.cloned.1.call-start = ((), (), s32[]{:S(2)}) async-start(), calls=%async_computation.2 | async-start | bytes 2162688 | tf_op jit(solution)/shard_map/all_gather | solution.py:20
  8.6 261.4 %reduce-scatter.4.cloned.1.call-start = ((), (), s32[]{:S(2)}) async-start(), calls=%async_computation.3 | async-start | bytes 2162688
Sparse Core Ops, SparseCore 0:
  10.1 98.0 all-gather.2
  111.4 55.7 all-gather.4
  172.2 97.8 reduce-scatter.3
where the time goes:
time: 277 us
  waiting for transfers between devices  245 us (88%)
  between operations  13.8 us (5%)
  matrix products  10.7 us (4%)
  local copies, waits for them, and re-layouts  5.87 us (2%)
    unnamed x4, waiting for transfers between devices  98.3 us
    all_gather x1, waiting for transfers between devices, shards(): lax.all_gather(grad_out, 'dp', axis=0, tiled=True)  96.5 us
    all_gather x1, waiting for transfers between devices, shards(): whole_input = lax.all_gather(activations, 'tensor', axis=0, tiled=True)  50.6 us
    dot_general x1, matrix products, shards(): lax.dot_general(whole_input, lax.all_gather(grad_out, 'dp', axis=0, tiled...  5.94 us
  transfers between devices with their start and end apart: 3, of which 3 were waited for; matrix products, arithmetic and copies ran while one was open for 6% of the time, Pallas kernels for 0%

commit v1 on v0

v1 whole, which is shorter than its diff:
```python
import math

import jax
import jax.numpy as jnp
from jax import lax
from jax.sharding import Mesh, PartitionSpec as P

AXES = ("z", "y_lo", "x", "y_hi", "core")
SIZES = (8, 2, 4, 4, 2)
PLANE = ("x", "y_hi")
SWAP = ((0, 1), (1, 0))


def expand_mask(block_mask, side, dtype):
    rows, cols = block_mask.shape
    flags = block_mask.astype(dtype)
    spread = jnp.broadcast_to(flags[:, None, :, None], (rows, side, cols, side))
    return spread.reshape(rows * side, cols * side)


def matmul(a, b, contract):
    return lax.dot_general(a, b, ((contract[:1], contract[1:]), ((), ())), preferred_element_type=jnp.float32)


def shards(activations, grad_out, weight, block_mask):
    side = weight.shape[0] // block_mask.shape[0]
    hidden = weight.shape[1]
    rows = activations.shape[0]
    chips = lax.axis_size("x") * lax.axis_size("y_hi")
    core = lax.axis_index("core")

    both = lax.all_gather(grad_out, "core", axis=0)
    own = lax.dynamic_slice(grad_out, (core * rows, 0), (rows, hidden))
    other = lax.dynamic_slice(both, (1 - core, core * rows, 0), (1, rows, hidden))[0]
    pair = jnp.concatenate([own, other], axis=1)
    pair = lax.all_gather(pair, "y_lo", axis=0, tiled=True)
    whole_out = lax.all_gather(pair, "z", axis=0, tiled=True)
    tokens = whole_out.shape[0] * 2

    masked = weight * expand_mask(block_mask, side, jnp.bfloat16)
    masked = jnp.concatenate([masked, lax.ppermute(masked, "core", SWAP)], axis=1)
    copies = jnp.broadcast_to(activations[None], (chips,) + activations.shape)
    inputs = lax.all_to_all(copies, PLANE, 0, 0, tiled=True)
    inputs = inputs.reshape(chips * rows, -1)

    partial_value = matmul(whole_out, masked, (1, 1)).astype(jnp.bfloat16)
    parts = lax.all_to_all(partial_value.reshape(chips, rows, -1), PLANE, 0, 0, tiled=True)
    grad_input = jnp.sum(parts.astype(jnp.float32), axis=0).astype(jnp.bfloat16)

    theirs = matmul(inputs, whole_out[:, hidden:], (0, 0)).astype(jnp.bfloat16)
    theirs = lax.ppermute(theirs, "core", SWAP)
    weight_sum = matmul(inputs, whole_out[:, :hidden], (0, 0)) + theirs.astype(jnp.float32)
    factor = 1.0 / math.sqrt(tokens)
    grad_weight = (weight_sum * expand_mask(block_mask, side, jnp.float32) * factor).astype(jnp.bfloat16)
    return (grad_input, grad_weight)


def solution(mesh):
    fine = Mesh(mesh.devices.reshape(SIZES), AXES)
    dp, tensor = ("z", "y_lo"), ("x", "y_hi", "core")
    return jax.shard_map(
        shards,
        mesh=fine,
        in_specs=(P(tensor, dp), P(dp, tensor), P(dp, tensor), P(dp, tensor)),
        out_specs=(P(tensor, dp), P(dp, tensor)),
        check_vma=False,
    )
```

time: 277 us -> 128 us (0.46)
  waiting for transfers between devices: 245 us -> 60.5 us
  starting transfers between devices: 0.11 us -> 23.6 us
  blocking collectives: 0 us -> 10.8 us
    all_gather x2 -> x1, waiting for transfers between devices: 147 us -> 41.4 us  [shards(): whole_out = lax.all_gather(pair, 'z', axis=0, tiled=True)]
    unnamed x4 -> x1, waiting for transfers between devices: 98.3 us -> 0.02 us
    all_to_all x0 -> x2, starting transfers between devices: none -> 19.8 us  [the longest x1 10.1 us: shards(): inputs = lax.all_to_all(copies, PLANE, 0, 0, tiled=True)]
    all_to_all x0 -> x2, waiting for transfers between devices: none -> 14.1 us  [the longest x1 14.1 us: shards(): lax.all_to_all(partial_value.reshape(chips, rows, -1), PLANE, 0, 0, tiled...]
    all_gather x0 -> x2, blocking collectives: none -> 10.8 us  [the longest x1 8.43 us: shards(): pair = lax.all_gather(pair, 'y_lo', axis=0, tiled=True)]
    ppermute x0 -> x2, waiting for transfers between devices: none -> 4.99 us  [the longest x1 2.56 us: shards(): theirs = lax.ppermute(theirs, 'core', SWAP)]
    ppermute x0 -> x2, starting transfers between devices: none -> 3.83 us  [the longest x1 1.92 us: shards(): lax.ppermute(masked, 'core', SWAP)]
    dot_general x2 -> x3, matrix products: 10.7 us -> 11.6 us  [matmul(): lax.dot_general(a, b, ((contract[:1], contract[1:]), ((), ())), preferred...]
  transfers between devices with their start and end apart: 3 -> 5, of which waited for: 3 -> 4; matrix products, arithmetic and copies ran while one was open for 6% -> 12% of each run, Pallas kernels for 0% -> 0%
where the time goes in v1:
time: 128 us; the launch traced here: 127 us
  waiting for transfers between devices  60.5 us (47%)
  starting transfers between devices  23.6 us (18%)
  between operations  14.1 us (11%)
  matrix products  11.6 us (9%)
  blocking collectives  10.8 us (8%)
  local copies, waits for them, and re-layouts  5.26 us (4%)
    all_gather x1, waiting for transfers between devices, shards(): whole_out = lax.all_gather(pair, 'z', axis=0, tiled=True)  41.4 us
    all_to_all x1, waiting for transfers between devices, shards(): lax.all_to_all(partial_value.reshape(chips, rows, -1), PLANE, 0, 0, tiled...  14.1 us
    dot_general x3, matrix products, matmul(): lax.dot_general(a, b, ((contract[:1], contract[1:]), ((), ())), preferred...  11.6 us
    all_to_all x1, starting transfers between devices, shards(): inputs = lax.all_to_all(copies, PLANE, 0, 0, tiled=True)  10.1 us
    all_to_all x1, starting transfers between devices, shards(): lax.all_to_all(partial_value.reshape(chips, rows, -1), PLANE, 0, 0, tiled...  9.72 us
    all_gather x1, blocking collectives, shards(): pair = lax.all_gather(pair, 'y_lo', axis=0, tiled=True)  8.43 us
  transfers between devices with their start and end apart: 5, of which 4 were waited for; matrix products, arithmetic and copies ran while one was open for 12% of the time, Pallas kernels for 0%

profile of v1, /device:TPU:6, one launch (start us, length us, event | category | flops | bytes accessed | tf_op | source)
XLA Modules:
  0.0 126.9 jit_solution(9998914938344607216)
XLA Ops:
  7.2 0.0 copy-start.1
  7.2 0.0 all-gather.3.cloned.1.call-start
  7.2 2.3 %all-gather = bf16[256,896]{1,0:T(8,128)(2,1)S(1)} all-gather(bf16[128,896]{1,0:T(8,128)(2,1)} %param.5), channel_id=2, replica_groups=mesh['z'=8,'y_lo'=2,'x'=4,'y_hi'=4,'core'=2] {'core'}, dimensions={0}, use_global_device_ids=true | all-gather | bytes 688128 | tf_op jit(solution)/shard_map/all_gather | solution.py:32
  9.6 0.9 constant_dynamic-slice_fusion
  10.5 8.4 %all_gather.14 = bf16[128,1792]{1,0:T(8,128)(2,1)} all-gather(bf16[64,1792]{1,0:T(8,128)(2,1)S(1)} %pad_maximum_fusion), channel_id=1, replica_groups=mesh['z'=8,'y_lo'=2,'x'=4,'y_hi'=4,'core'=2] {'y_lo'}, dimensions={0}, use_global_device_ids=true | all-gather | bytes 688128 | tf_op jit(solution)/shard_map/all_gather | solution.py:36
  19.0 0.0 copy-start.2
  19.0 0.0 all-gather.3.cloned.1.call-update
  19.0 0.0 copy-done.1
  19.0 1.1 broadcast_in_dim.7
  20.1 10.1 %all-to-all-start.1 = ((bf16[16,64,512]{2,1,0:T(8,128)(2,1)}), bf16[16,64,512]{2,1,0:T(8,128)(2,1)S(1)}, u32[]{:S(2)}, u32[]{:S(2)}) async-start(bf16[16,64,512]{2,1,0:T(8,128)(2,1)} %broadcast_in_dim.7), calls=%async_computation.1 | async-start | bytes 2097152 | tf_op jit(solution)/shard_map/all_to_all | solution.py:43
  30.2 0.0 copy-done.2
  30.2 0.1 copy.8
  30.3 0.0 copy-done
  30.3 0.5 copy.9
  30.8 0.3 broadcast_in_dim.6
  31.1 0.2 bitcast_multiply_fusion.1
  31.3 1.9 %collective-permute-start = (bf16[512,896]{0,1:T(8,128)(2,1)S(1)}, bf16[512,896]{0,1:T(8,128)(2,1)S(1)}, u32[]{:S(2)}, u32[]{:S(2)}) collective-permute-start(bf16[512,896]{0,1:T(8,128)(2,1)S(1)} %bitcast_multiply_fusion.1), channel_id=1, source_target_pairs={{0,1},{1,0},{2,3},{3,2},{4,5},{5,4},{6,7},{7,6},{8,9},{9,8},{10,11... | collective-permute-start | bytes 2752520 | tf_op jit(solution)/shard_map/ppermute | solution.py:41
  33.2 2.4 %collective-permute-done = bf16[512,896]{0,1:T(8,128)(2,1)S(1)} collective-permute-done((bf16[512,896]{0,1:T(8,128)(2,1)S(1)}, bf16[512,896]{0,1:T(8,128)(2,1)S(1)}, u32[]{:S(2)}, u32[]{:S(2)}) %collective-permute-start) | collective-permute-done | bytes 917536 | tf_op jit(solution)/shard_map/ppermute | solution.py:41
  35.7 41.4 %all-gather.3.cloned.1.call-done = bf16[1024,1792]{1,0:T(8,128)(2,1)} async-done(((bf16[128,1792]{1,0:T(8,128)(2,1)}), bf16[1024,1792]{1,0:T(8,128)(2,1)}) %all-gather.3.cloned.1.call-update) | async-done | bytes 3670032 | tf_op jit(solution)/shard_map/all_gather | solution.py:37
  77.1 5.1 %fusion.12 = bf16[1024,512]{1,0:T(8,128)(2,1)} fusion(bf16[1024,1792]{1,0:T(8,128)(2,1)} %all-gather.3.cloned.1.call-done, bf16[512,896]{0,1:T(8,128)(2,1)S(1)} %collective-permute-done, bf16[512,896]{0,1:T(8,128)(2,1)S(1)} %bitcast_multiply_fusion.1), kind=kOutput, calls=%fused_computation.12 | convolution fusion | flops 1883242496 | bytes 6553600 | tf_op jit(solution)/shard_map/dot_general | solution.py:22
  82.2 0.0 all-to-all-done.1
  82.2 9.7 %all-to-all-start = ((bf16[16,64,512]{2,1,0:T(8,128)(2,1)}), bf16[16,64,512]{2,1,0:T(8,128)(2,1)S(1)}, u32[]{:S(2)}, u32[]{:S(2)}) async-start(bf16[16,64,512]{2,1,0:T(8,128)(2,1)} %bitcast.2), calls=%async_computation | async-start | bytes 2097152 | tf_op jit(solution)/shard_map/all_to_all | solution.py:47
  91.9 3.6 %fusion.18 = bf16[512,896]{0,1:T(8,128)(2,1)} fusion(bf16[1024,512]{1,0:T(8,128)(2,1)S(1)} %bitcast.32, bf16[1024,1792]{1,0:T(8,128)(2,1)} %all-gather.3.cloned.1.call-done), kind=kOutput, calls=%fused_computation.14 | convolution fusion | flops 939982848 | bytes 3801088 | tf_op jit(solution)/shard_map/dot_general | solution.py:22
  95.5 1.9 %collective-permute-start.1 = (bf16[512,896]{0,1:T(8,128)(2,1)}, bf16[512,896]{0,1:T(8,128)(2,1)S(1)}, u32[]{:S(2)}, u32[]{:S(2)}) collective-permute-start(bf16[512,896]{0,1:T(8,128)(2,1)} %fusion.18), channel_id=1, source_target_pairs={{0,1},{1,0},{2,3},{3,2},{4,5},{5,4},{6,7},{7,6},{8,9},{9,8},{10,11... | collective-permute-start | bytes 2752520 | tf_op jit(solution)/shard_map/ppermute | solution.py:51
  97.4 0.1 copy.10
  97.5 2.6 %collective-permute-done.1 = bf16[512,896]{0,1:T(8,128)(2,1)S(1)} collective-permute-done((bf16[512,896]{0,1:T(8,128)(2,1)}, bf16[512,896]{0,1:T(8,128)(2,1)S(1)}, u32[]{:S(2)}, u32[]{:S(2)}) %collective-permute-start.1) | collective-permute-done | bytes 917536 | tf_op jit(solution)/shard_map/ppermute | solution.py:51
  100.0 0.3 broadcast_in_dim.8
  100.3 0.6 copy-done.3
  100.9 2.9 %fusion.1 = bf16[512,896]{0,1:T(8,128)(2,1)S(1)} fusion(f32[112,8,4,128]{3,2,1,0:T(4,128)S(1)} %bitcast.31, bf16[512,896]{0,1:T(8,128)(2,1)} %copy-done.3, bf16[1024,512]{1,0:T(8,128)(2,1)S(1)} %bitcast.33, bf16[1024,1792]{1,0:T(8,128)(2,1)} %all-gather.3.cloned.1.call-done), kind=kOutput, calls=%fused_computation.2 | convolution fusion | flops 941817856 | bytes 6553600 | tf_op jit(solution)/shard_map/dot_general | solution.py:22
  103.9 1.3 %copy.11 = bf16[512,896]{1,0:T(8,128)(2,1)} copy(bf16[512,896]{0,1:T(8,128)(2,1)S(1)} %fusion.1) | data formatting | bytes 1835008
  105.1 14.1 %all-to-all-done = bf16[16,64,512]{2,1,0:T(8,128)(2,1)S(1)} async-done(((bf16[16,64,512]{2,1,0:T(8,128)(2,1)}), bf16[16,64,512]{2,1,0:T(8,128)(2,1)S(1)}, u32[]{:S(2)}, u32[]{:S(2)}) %all-to-all-start) | async-done | bytes 1048608 | tf_op jit(solution)/shard_map/all_to_all | solution.py:47
  119.3 0.8 reduce_sum.12
  (5 shorter events, 0.1 us)
Async XLA Ops:
  7.2 11.8 %copy-start.1 = (bf16[64,512]{1,0:T(8,128)(2,1)S(1)}, bf16[64,512]{1,0:T(8,128)(2,1)}, u32[]{:S(2)}) copy-start(bf16[64,512]{1,0:T(8,128)(2,1)} %param.4) | copy-start | bytes 196612
  7.2 69.9 %all-gather.3.cloned.1.call-start = ((), (), s32[]{:S(2)}) async-start(), calls=%async_computation.2 | async-start | bytes 4128768 | tf_op jit(solution)/shard_map/all_gather | solution.py:37
  19.0 11.2 %copy-start.2 = (s32[4,7]{1,0:T(4,128)S(1)}, s32[4,7]{1,0:T(4,128)}, u32[]{:S(2)}) copy-start(s32[4,7]{1,0:T(4,128)} %param.7) | copy-start | bytes 340
  19.0 11.3 %copy-start = (bf16[512,896]{1,0:T(8,128)(2,1)S(1)}, bf16[512,896]{1,0:T(8,128)(2,1)}, u32[]{:S(2)}) copy-start(bf16[512,896]{1,0:T(8,128)(2,1)} %param.6) | copy-start | bytes 2752516
  20.1 62.1 %all-to-all-start.1 = ((bf16[16,64,512]{2,1,0:T(8,128)(2,1)}), bf16[16,64,512]{2,1,0:T(8,128)(2,1)S(1)}, u32[]{:S(2)}, u32[]{:S(2)}) async-start(bf16[16,64,512]{2,1,0:T(8,128)(2,1)} %broadcast_in_dim.7), calls=%async_computation.1 | async-start | bytes 2097152 | tf_op jit(solution)/shard_map/all_to_all | solution.py:43
  31.3 4.4 %collective-permute-start = (bf16[512,896]{0,1:T(8,128)(2,1)S(1)}, bf16[512,896]{0,1:T(8,128)(2,1)S(1)}, u32[]{:S(2)}, u32[]{:S(2)}) collective-permute-start(bf16[512,896]{0,1:T(8,128)(2,1)S(1)} %bitcast_multiply_fusion.1), channel_id=1, source_target_pairs={{0,1},{1,0},{2,3},{3,2},{4,5},{5,4},{6,7},{7,6},{8,9},{9,8},{10,11... | collective-permute-start | bytes 2752520 | tf_op jit(solution)/shard_map/ppermute | solution.py:41
  82.2 37.1 %all-to-all-start = ((bf16[16,64,512]{2,1,0:T(8,128)(2,1)}), bf16[16,64,512]{2,1,0:T(8,128)(2,1)S(1)}, u32[]{:S(2)}, u32[]{:S(2)}) async-start(bf16[16,64,512]{2,1,0:T(8,128)(2,1)} %bitcast.2), calls=%async_computation | async-start | bytes 2097152 | tf_op jit(solution)/shard_map/all_to_all | solution.py:47
  95.5 4.6 %collective-permute-start.1 = (bf16[512,896]{0,1:T(8,128)(2,1)}, bf16[512,896]{0,1:T(8,128)(2,1)S(1)}, u32[]{:S(2)}, u32[]{:S(2)}) collective-permute-start(bf16[512,896]{0,1:T(8,128)(2,1)} %fusion.18), channel_id=1, source_target_pairs={{0,1},{1,0},{2,3},{3,2},{4,5},{5,4},{6,7},{7,6},{8,9},{9,8},{10,11... | collective-permute-start | bytes 2752520 | tf_op jit(solution)/shard_map/ppermute | solution.py:51
  100.0 0.9 copy-start.3
Sparse Core Ops, SparseCore 0:
  19.1 57.9 all-gather.2

commit v2 on v1

v2 whole, which is shorter than its diff:
```python
import functools
import math

import jax
import jax.numpy as jnp
from jax import lax
from jax.experimental import pallas as pl
from jax.experimental.pallas import tpu as pltpu
from jax.sharding import Mesh, PartitionSpec as P

AXES = ("z", "y_lo", "x", "y_hi", "core")
SIZES = (8, 2, 4, 4, 2)
SWAP = ((0, 1), (1, 0))


def expand_mask(block_mask, side, dtype):
    rows, cols = block_mask.shape
    flags = block_mask.astype(dtype)
    spread = jnp.broadcast_to(flags[:, None, :, None], (rows, side, cols, side))
    return spread.reshape(rows * side, cols * side)


def matmul(a, b, contract):
    return lax.dot_general(a, b, ((contract[:1], contract[1:]), ((), ())), preferred_element_type=jnp.float32)


def near(place, size):
    return place ^ 1


def next_pair(place, size):
    return (((place - 1 + size) % size ^ 1) + 1) % size


def swap(value, axis, partner):
    size = lax.axis_size(axis)
    pairs = []
    for place in range(size):
        for core in range(2):
            there = (partner((place - core) % size, size) + core) % size
            pairs.append((place * 2 + core, there * 2 + core))
    return lax.ppermute(value, (axis, "core"), pairs)


def after(value, *done):
    return lax.optimization_barrier((value,) + done)[0]


def call(kernel, outs, args, n_scalar, scratch=()):
    scalar, vector = pl.BlockSpec(memory_space=pltpu.SMEM), pl.BlockSpec(memory_space=pltpu.VMEM)
    return pl.pallas_call(
        kernel,
        out_shape=[jax.ShapeDtypeStruct(shape, jnp.bfloat16) for shape in outs],
        in_specs=[scalar] * n_scalar + [vector] * (len(args) - n_scalar),
        out_specs=[vector] * len(outs),
        scratch_shapes=list(scratch),
        compiler_params=pltpu.CompilerParams(vmem_limit_bytes=24 * 2**20),
    )(*args)


def dot(a, b, contract):
    return lax.dot_general(a, b, ((contract[:1], contract[1:]), ((), ())), preferred_element_type=jnp.float32)


def block_at(index, rows):
    return pl.ds(pl.multiple_of(index * rows, rows), rows)


def place_kernel(order, *refs):
    parts, out = refs[:-1], refs[-1]
    rows = parts[0].shape[0] // 2
    for k, part in enumerate(parts):
        for i in range(2):
            out[block_at(order[2 * k + i], rows)] = part[i * rows : (i + 1) * rows]


def away_kernel(order, quad, *refs):
    parts, in_rows, away, held = refs[:-3], refs[-3], refs[-2], refs[-1]
    rows, hidden = quad.shape[1], away.shape[1]
    for k, part in enumerate(parts):
        held[2 * k * rows : (2 * k + 2) * rows] = part[:, hidden:]
        for i in range(2 * k, 2 * k + 2):
            in_rows[i * rows : (i + 1) * rows] = quad[order[i]]
    away[...] = dot(in_rows[...], held[...], (0, 0)).astype(jnp.bfloat16)


def home_kernel(factor, mask, in_rows, received, *refs):
    parts, out, held = refs[:-2], refs[-2], refs[-1]
    width, hidden = out.shape
    rows = parts[0].shape[0]
    for k, part in enumerate(parts):
        held[k * rows : (k + 1) * rows] = part[:, :hidden]
    height, side = width // mask.shape[0], hidden // mask.shape[1]
    total = dot(in_rows[...], held[...], (0, 0)) + received[...].astype(jnp.float32)
    for i in range(mask.shape[0]):
        for j in range(mask.shape[1]):
            keep = mask[i, j].astype(jnp.float32)
            block = total[i * height : (i + 1) * height, j * side : (j + 1) * side]
            out[i * height : (i + 1) * height, j * side : (j + 1) * side] = (block * keep * factor).astype(jnp.bfloat16)


def shards(activations, grad_out, weight, block_mask):
    side = weight.shape[0] // block_mask.shape[0]
    width, hidden = weight.shape
    rows = activations.shape[0]
    core = lax.axis_index("core")
    z, r = lax.axis_index("z"), lax.axis_index("y_lo")

    here = (z - core) % 8
    other, one = here ^ 1, next_pair(here, 8)
    two, far = next_pair(other, 8), next_pair(one ^ 1, 8)
    ring = [here, other, one, one ^ 1, two, two ^ 1, far, far ^ 1]
    three = two ^ 1
    ring += [here, one, other, two, one ^ 1, next_pair(one ^ 1, 8), three, next_pair(three, 8)]
    spots = [(s + core) % 8 for s in ring]
    chips = [spot // 2 * 4 + spot % 2 * 2 + (r if i < 8 else 1 - r) for i, spot in enumerate(spots)]
    order = jnp.stack(chips).astype(jnp.int32)

    both = lax.all_gather(grad_out, "core", axis=0)
    own = lax.dynamic_slice(grad_out, (core * rows, 0), (rows, hidden))
    sibling = lax.dynamic_slice(both, (1 - core, core * rows, 0), (1, rows, hidden))[0]
    first = jnp.concatenate([own, sibling], axis=1)

    across = lax.ppermute(first, "y_lo", SWAP)
    a1 = swap(first, "z", near)
    a1 = jnp.concatenate([first, a1], axis=0)
    a2 = swap(a1, "z", next_pair)
    b1 = swap(across, "z", next_pair)
    b1 = jnp.concatenate([across, b1], axis=0)
    masked = after(weight, across) * expand_mask(block_mask, side, jnp.bfloat16)
    wide = jnp.concatenate([masked, lax.ppermute(masked, "core", SWAP)], axis=1)
    wide = lax.optimization_barrier(wide)
    b2 = swap(b1, "z", near)
    copies = jnp.broadcast_to(after(activations, a1)[None], (16,) + activations.shape)
    quad = lax.all_to_all(copies, ("x", "y_hi"), 0, 0, tiled=True)
    a3 = swap(a2, "z", near)
    b3 = swap(b2, "z", next_pair)
    a4 = swap(a3, "z", next_pair)
    b4 = swap(b3, "z", near)

    parts = (a1, a2, a3, a4, b1, b2, b3, b4)
    value = [matmul(part, wide, (1, 1)).astype(jnp.bfloat16) for part in parts]
    (value,) = call(place_kernel, [(16 * rows, width)], (order, *value), 1)
    value = lax.all_to_all(value.reshape(16, rows, width), ("x", "y_hi"), 0, 0, tiled=True)
    grad_input = jnp.sum(value.astype(jnp.float32), axis=0).astype(jnp.bfloat16)

    scratch = [pltpu.VMEM((16 * rows, hidden), jnp.bfloat16)]
    in_rows, away = call(away_kernel, [(16 * rows, width), (width, hidden)], (order, quad, *parts), 1, scratch)
    received = lax.ppermute(away, "core", SWAP)
    factor = 1.0 / math.sqrt(rows * 32)
    home = functools.partial(home_kernel, factor)
    (grad_weight,) = call(home, [(width, hidden)], (block_mask, in_rows, received, *parts), 1, scratch)
    return (grad_input, grad_weight)


def solution(mesh):
    fine = Mesh(mesh.devices.reshape(SIZES), AXES)
    dp, tensor = ("z", "y_lo"), ("x", "y_hi", "core")
    return jax.shard_map(
        shards,
        mesh=fine,
        in_specs=(P(tensor, dp), P(dp, tensor), P(dp, tensor), P(dp, tensor)),
        out_specs=(P(tensor, dp), P(dp, tensor)),
        check_vma=False,
    )
```

time: 128 us -> 126 us (0.984)
  starting transfers between devices: 23.6 us -> 61.9 us
  waiting for transfers between devices: 60.5 us -> 36.7 us
  between operations: 14.1 us -> 1.62 us
  matrix products: 11.6 us -> 3.25 us
  blocking collectives: 10.8 us -> 2.48 us
  Pallas kernels: 0 us -> 6.27 us
  other arithmetic: 0.97 us -> 5.38 us
  local copies, waits for them, and re-layouts: 5.26 us -> 7.11 us
    all_gather x1 -> x0, waiting for transfers between devices: 41.4 us -> none  [shards(): whole_out = lax.all_gather(pair, 'z', axis=0, tiled=True)]
    ppermute x2 -> x11, starting transfers between devices: 3.83 us -> 42.2 us  [the longest x8 29.4 us: swap(): return lax.ppermute(value, (axis, 'core'), pairs)]
    ppermute x2 -> x11, waiting for transfers between devices: 4.99 us -> 22.1 us  [the longest x8 18.7 us: swap(): return lax.ppermute(value, (axis, 'core'), pairs)]
    all_gather x1 -> x0, blocking collectives: 8.43 us -> none  [shards(): pair = lax.all_gather(pair, 'y_lo', axis=0, tiled=True)]
    dot_general x3 -> x8, matrix products: 11.6 us -> 3.25 us  [matmul(): lax.dot_general(a, b, ((contract[:1], contract[1:]), ((), ())), preferred...]
    pallas_call x0 -> x3, Pallas kernels: none -> 6.27 us  [call(): pl.pallas_call(kernel, out_shape=[jax.ShapeDtypeStruct(shape, jnp.bfloat1...]
    concatenate x1 -> x3, other arithmetic: 0.02 us -> 1.63 us  [the longest x1 1.58 us: shards(): wide = jnp.concatenate([masked, lax.ppermute(masked, 'core', SWAP)], axis=1)]
    unnamed x10 -> x31, local copies, waits for them, and re-layouts: 2.43 us -> 4.02 us
  transfers between devices with their start and end apart: 5 -> 13, of which waited for: 4 -> 7; matrix products, arithmetic and copies ran while one was open for 12% -> 7% of each run, Pallas kernels for 0% -> 5%
where the time goes in v2:
time: 126 us; the launch traced here: 125 us
  starting transfers between devices  61.9 us (49%)
  waiting for transfers between devices  36.7 us (29%)
  local copies, waits for them, and re-layouts  7.11 us (6%)
  Pallas kernels  6.27 us (5%)
  other arithmetic  5.38 us (4%)
  matrix products  3.25 us (3%)
  blocking collectives  2.48 us (2%)
  between operations  1.62 us (1%)
    ppermute x8, starting transfers between devices, swap(): return lax.ppermute(value, (axis, 'core'), pairs)  29.4 us
    ppermute x8, waiting for transfers between devices, swap(): return lax.ppermute(value, (axis, 'core'), pairs)  18.7 us
    all_to_all x1, waiting for transfers between devices, shards(): lax.all_to_all(value.reshape(16, rows, width), ('x', 'y_hi'), 0, 0, tiled...  14.5 us
    all_to_all x1, starting transfers between devices, shards(): quad = lax.all_to_all(copies, ('x', 'y_hi'), 0, 0, tiled=True)  10.1 us
    all_to_all x1, starting transfers between devices, shards(): lax.all_to_all(value.reshape(16, rows, width), ('x', 'y_hi'), 0, 0, tiled...  9.64 us
    ppermute x1, starting transfers between devices, shards(): wide = jnp.concatenate([masked, lax.ppermute(masked, 'core', SWAP)], axis=1)  7.32 us
    pallas_call x3, Pallas kernels, call(): pl.pallas_call(kernel, out_shape=[jax.ShapeDtypeStruct(shape, jnp.bfloat1...  6.27 us
    unnamed x31, local copies, waits for them, and re-layouts  4.02 us
  transfers between devices with their start and end apart: 13, of which 7 were waited for; matrix products, arithmetic and copies ran while one was open for 7% of the time, Pallas kernels for 5%

profile of v2, /device:TPU:6, one launch (start us, length us, event | category | flops | bytes accessed | tf_op | source)
XLA Modules:
  0.0 124.6 jit_solution(301754105135992760)
XLA Ops:
  0.6 2.5 %all-gather = bf16[256,896]{1,0:T(8,128)(2,1)S(1)} all-gather(bf16[128,896]{1,0:T(8,128)(2,1)} %param.5), channel_id=2, replica_groups=mesh['z'=8,'y_lo'=2,'x'=4,'y_hi'=4,'core'=2] {'core'}, dimensions={0}, use_global_device_ids=true | all-gather | bytes 688128 | tf_op jit(solution)/shard_map/all_gather | solution.py:119
  3.1 0.9 constant_dynamic-slice_fusion
  4.1 3.5 %collective-permute-start.1 = (bf16[64,1792]{1,0:T(8,128)(2,1)S(1)}, bf16[64,1792]{1,0:T(8,128)(2,1)S(1)}, u32[]{:S(2)}, u32[]{:S(2)}) collective-permute-start(bf16[64,1792]{1,0:T(8,128)(2,1)S(1)} %pad_maximum_fusion.2), channel_id=1, source_target_pairs={{0,32},{32,0},{1,33},{33,1},{2,34},{34,2},{3,35},{35,3},{4,36},{36... | collective-permute-start | bytes 688136 | tf_op jit(solution)/shard_map/ppermute | solution.py:124
  7.6 4.3 %collective-permute-start = (bf16[64,1792]{1,0:T(8,128)(2,1)S(1)}, bf16[64,1792]{1,0:T(8,128)(2,1)S(1)}, u32[]{:S(2)}, u32[]{:S(2)}) collective-permute-start(bf16[64,1792]{1,0:T(8,128)(2,1)S(1)} %pad_maximum_fusion.2), channel_id=1, source_target_pairs={{0,64},{1,449},{64,0},{65,129},{128,192},{129,65},{192,128},{193,2... | collective-permute-start | bytes 688136 | tf_op jit(solution)/shard_map/ppermute | solution.py:42
  12.7 1.0 collective-permute-done.1
  14.5 1.0 bitcast_multiply_fusion
  15.5 7.3 %collective-permute-start.2 = (bf16[512,896]{0,1:T(8,128)(2,1)}, bf16[512,896]{0,1:T(8,128)(2,1)}, u32[]{:S(2)}, u32[]{:S(2)}) collective-permute-start(bf16[512,896]{0,1:T(8,128)(2,1)} %bitcast_multiply_fusion), channel_id=1, source_target_pairs={{0,1},{1,0},{2,3},{3,2},{4,5},{5,4},{6,7},{7,6},{8,9},{9,8},{10,11... | collective-permute-start | bytes 2752520 | tf_op jit(solution)/shard_map/ppermute | solution.py:131
  22.9 5.7 %collective-permute-start.3 = (bf16[128,1792]{1,0:T(8,128)(2,1)S(1)}, bf16[128,1792]{1,0:T(8,128)(2,1)S(1)}, u32[]{:S(2)}, u32[]{:S(2)}) collective-permute-start(bf16[128,1792]{1,0:T(8,128)(2,1)S(1)} %pad_maximum_fusion.1.refs_0_), channel_id=1, source_target_pairs={{0,448},{1,65},{64,128},{65,1},{128,64},{129,193},{192,256},{193,1... | collective-permute-start | bytes 1376264 | tf_op jit(solution)/shard_map/ppermute | solution.py:42
  28.6 1.9 %collective-permute-start.6 = (bf16[64,1792]{1,0:T(8,128)(2,1)S(1)}, bf16[64,1792]{1,0:T(8,128)(2,1)S(1)}, u32[]{:S(2)}, u32[]{:S(2)}) collective-permute-start(bf16[64,1792]{1,0:T(8,128)(2,1)S(1)} %collective-permute-done.1), channel_id=1, source_target_pairs={{0,448},{1,65},{64,128},{65,1},{128,64},{129,193},{192,256},{193,1... | collective-permute-start | bytes 688136 | tf_op jit(solution)/shard_map/ppermute | solution.py:42
  30.6 7.2 %collective-permute-done.6 = bf16[64,1792]{1,0:T(8,128)(2,1)S(1)} collective-permute-done((bf16[64,1792]{1,0:T(8,128)(2,1)S(1)}, bf16[64,1792]{1,0:T(8,128)(2,1)S(1)}, u32[]{:S(2)}, u32[]{:S(2)}) %collective-permute-start.6) | collective-permute-done | bytes 229408 | tf_op jit(solution)/shard_map/ppermute | solution.py:42
  37.8 1.9 %collective-permute-start.7 = (bf16[128,1792]{1,0:T(8,128)(2,1)S(1)}, bf16[128,1792]{1,0:T(8,128)(2,1)S(1)}, u32[]{:S(2)}, u32[]{:S(2)}) collective-permute-start(bf16[128,1792]{1,0:T(8,128)(2,1)S(1)} %constant_dynamic-update-slice_fusion.refs_4_), channel_id=1, source_target_pairs={{0,64},{1,449},{64,0},{65,129},{128,192},{129,65},{192,128},{193,2... | collective-permute-start | bytes 1376264 | tf_op jit(solution)/shard_map/ppermute | solution.py:42
  40.4 1.1 broadcast_in_dim.5
  41.5 10.1 %all-to-all-start.1 = ((bf16[16,64,512]{2,1,0:T(8,128)(2,1)}), bf16[16,64,512]{2,1,0:T(8,128)(2,1)S(1)}, u32[]{:S(2)}, u32[]{:S(2)}) async-start(bf16[16,64,512]{2,1,0:T(8,128)(2,1)} %broadcast_in_dim.5), calls=%async_computation.1 | async-start | bytes 2097152 | tf_op jit(solution)/shard_map/all_to_all | solution.py:135
  51.6 3.9 %collective-permute-start.4 = (bf16[128,1792]{1,0:T(8,128)(2,1)S(1)}, bf16[128,1792]{1,0:T(8,128)(2,1)S(1)}, u32[]{:S(2)}, u32[]{:S(2)}) collective-permute-start(bf16[128,1792]{1,0:T(8,128)(2,1)S(1)} %collective-permute-done.3.refs_1_), channel_id=1, source_target_pairs={{0,64},{1,449},{64,0},{65,129},{128,192},{129,65},{192,128},{193,2... | collective-permute-start | bytes 1376264 | tf_op jit(solution)/shard_map/ppermute | solution.py:42
  55.5 4.9 %collective-permute-start.8 = (bf16[128,1792]{1,0:T(8,128)(2,1)S(1)}, bf16[128,1792]{1,0:T(8,128)(2,1)S(1)}, u32[]{:S(2)}, u32[]{:S(2)}) collective-permute-start(bf16[128,1792]{1,0:T(8,128)(2,1)S(1)} %collective-permute-done.7.refs_5_), channel_id=1, source_target_pairs={{0,448},{1,65},{64,128},{65,1},{128,64},{129,193},{192,256},{193,1... | collective-permute-start | bytes 1376264 | tf_op jit(solution)/shard_map/ppermute | solution.py:42
  60.5 1.6 %pad_maximum_fusion = bf16[512,1792]{0,1:T(8,128)(2,1)S(1)} fusion(bf16[512,896]{0,1:T(8,128)(2,1)} %collective-permute-done.2, bf16[512,896]{0,1:T(8,128)(2,1)} %bitcast_multiply_fusion), kind=kLoop, calls=%fused_computation | loop fusion | flops 3670016 | bytes 3670016 | tf_op jit(solution)/shard_map/concatenate | solution.py:131
  62.5 4.0 %collective-permute-done.4.refs_2_ = bf16[128,1792]{1,0:T(8,128)(2,1)S(1)} collective-permute-done((bf16[128,1792]{1,0:T(8,128)(2,1)S(1)}, bf16[128,1792]{1,0:T(8,128)(2,1)S(1)}, u32[]{:S(2)}, u32[]{:S(2)}) %collective-permute-start.4) | collective-permute-done | bytes 458784 | tf_op jit(solution)/shard_map/ppermute | solution.py:42
  66.4 4.9 %collective-permute-start.5 = (bf16[128,1792]{1,0:T(8,128)(2,1)S(1)}, bf16[128,1792]{1,0:T(8,128)(2,1)S(1)}, u32[]{:S(2)}, u32[]{:S(2)}) collective-permute-start(bf16[128,1792]{1,0:T(8,128)(2,1)S(1)} %collective-permute-done.4.refs_2_), channel_id=1, source_target_pairs={{0,448},{1,65},{64,128},{65,1},{128,64},{129,193},{192,256},{193,1... | collective-permute-start | bytes 1376264 | tf_op jit(solution)/shard_map/ppermute | solution.py:42
  73.2 1.9 %collective-permute-start.9 = (bf16[128,1792]{1,0:T(8,128)(2,1)S(1)}, bf16[128,1792]{1,0:T(8,128)(2,1)S(1)}, u32[]{:S(2)}, u32[]{:S(2)}) collective-permute-start(bf16[128,1792]{1,0:T(8,128)(2,1)S(1)} %collective-permute-done.8.refs_6_), channel_id=1, source_target_pairs={{0,64},{1,449},{64,0},{65,129},{128,192},{129,65},{192,128},{193,2... | collective-permute-start | bytes 1376264 | tf_op jit(solution)/shard_map/ppermute | solution.py:42
  75.5 7.2 %collective-permute-done.5.refs_3_ = bf16[128,1792]{1,0:T(8,128)(2,1)S(1)} collective-permute-done((bf16[128,1792]{1,0:T(8,128)(2,1)S(1)}, bf16[128,1792]{1,0:T(8,128)(2,1)S(1)}, u32[]{:S(2)}, u32[]{:S(2)}) %collective-permute-start.5) | collective-permute-done | bytes 458784 | tf_op jit(solution)/shard_map/ppermute | solution.py:42
  84.0 0.8 copy-done.5
  84.7 1.6 %shard_map.59 = bf16[1024,512]{1,0:T(8,128)(2,1)} custom-call(s32[16]{0:T(128)S(1)} %stack.67.order, bf16[128,512]{1,0:T(8,128)(2,1)S(1)} %convolution_convert_fusion.7.refs_0_, bf16[128,512]{1,0:T(8,128)(2,1)S(1)} %convolution_convert_fusion.6.refs_1_, bf16[128,512]{1,0:T(8,128)(2,1)S(1)} %convolution_convert_fusion.5.refs_2_, ...), custom_call_target="tpu_custom_call" | custom-call | tf_op jit(solution)/shard_map/pallas_call | solution.py:51
  86.3 9.6 %all-to-all-start = ((bf16[16,64,512]{2,1,0:T(8,128)(2,1)}), bf16[16,64,512]{2,1,0:T(8,128)(2,1)}, u32[]{:S(2)}, u32[]{:S(2)}) async-start(bf16[16,64,512]{2,1,0:T(8,128)(2,1)} %bitcast.18), calls=%async_computation | async-start | bytes 2097152 | tf_op jit(solution)/shard_map/all_to_all | solution.py:144
  95.9 1.0 copy-done.1
  97.0 1.0 copy-done.4
  98.0 1.0 copy-done.6
  99.0 1.9 %shard_map.60 = (bf16[1024,512]{1,0:T(8,128)(2,1)S(1)}, bf16[512,896]{1,0:T(8,128)(2,1)S(1)}) custom-call(s32[16]{0:T(128)S(1)} %stack.67.order, bf16[16,64,512]{2,1,0:T(8,128)(2,1)S(1)} %all-to-all-done.1.quad, bf16[128,1792]{1,0:T(8,128)(2,1)S(1)} %pad_maximum_fusion.1.refs_0_, bf16[128,1792]{1,0:T(8,128)(2,1)S(1)} %collective-permute-done.3.refs_1_, ...), custom_call_target="tpu_custom_call" | custom-call | tf_op jit(solution)/shard_map/pallas_call | solution.py:51
  100.9 1.9 %collective-permute-start.10 = (bf16[512,896]{1,0:T(8,128)(2,1)S(1)}, bf16[512,896]{1,0:T(8,128)(2,1)S(1)}, u32[]{:S(2)}, u32[]{:S(2)}) collective-permute-start(bf16[512,896]{1,0:T(8,128)(2,1)S(1)} %get-tuple-element.9), channel_id=1, source_target_pairs={{0,1},{1,0},{2,3},{3,2},{4,5},{5,4},{6,7},{7,6},{8,9},{9,8},{10,11... | collective-permute-start | bytes 2752520 | tf_op jit(solution)/shard_map/ppermute | solution.py:149
  102.8 2.4 %collective-permute-done.10.received = bf16[512,896]{1,0:T(8,128)(2,1)S(1)} collective-permute-done((bf16[512,896]{1,0:T(8,128)(2,1)S(1)}, bf16[512,896]{1,0:T(8,128)(2,1)S(1)}, u32[]{:S(2)}, u32[]{:S(2)}) %collective-permute-start.10) | collective-permute-done | bytes 917536 | tf_op jit(solution)/shard_map/ppermute | solution.py:149
  105.2 2.8 %shard_map.61 = bf16[512,896]{1,0:T(8,128)(2,1)} custom-call(s32[4,7]{1,0:T(4,128)S(1)} %copy-done.8, bf16[1024,512]{1,0:T(8,128)(2,1)S(1)} %get-tuple-element.8.in_rows, bf16[512,896]{1,0:T(8,128)(2,1)S(1)} %collective-permute-done.10.received, bf16[128,1792]{1,0:T(8,128)(2,1)S(1)} %pad_maximum_fusion.1.refs_0_, ...), custom_call_target="tpu_custom_call" | custom-call | tf_op jit(solution)/shard_map/pallas_call | solution.py:51
  108.1 14.5 %all-to-all-done = bf16[16,64,512]{2,1,0:T(8,128)(2,1)} async-done(((bf16[16,64,512]{2,1,0:T(8,128)(2,1)}), bf16[16,64,512]{2,1,0:T(8,128)(2,1)}, u32[]{:S(2)}, u32[]{:S(2)}) %all-to-all-start) | async-done | bytes 1048608 | tf_op jit(solution)/shard_map/all_to_all | solution.py:144
  122.6 2.0 %reduce_sum.12 = bf16[64,512]{1,0:T(8,128)(2,1)} reduce(bf16[16,64,512]{2,1,0:T(8,128)(2,1)} %all-to-all-done, bf16[]{:T(256)} %constant.270.clone.1), dimensions={0}, to_apply=%region_0.1 | reduce | flops 491520 | bytes 1114114 | tf_op jit(solution)/shard_map/reduce_sum | solution.py:145
  (51 shorter events, 5.7 us)
Async XLA Ops:
  0.6 13.0 %copy-start.11 = (bf16[512,896]{1,0:T(8,128)(2,1)S(1)}, bf16[512,896]{1,0:T(8,128)(2,1)}, u32[]{:S(2)}) copy-start(bf16[512,896]{1,0:T(8,128)(2,1)} %param.6) | copy-start | bytes 2752516
  4.1 18.8 %copy-start.9 = (bf16[64,896]{1,0:T(8,128)(2,1)}, bf16[64,896]{1,0:T(8,128)(2,1)S(1)}, u32[]{:S(2)}) copy-start(bf16[64,896]{1,0:T(8,128)(2,1)S(1)} %dynamic-slice_bitcast_fusion) | copy-start | bytes 344068
  4.1 9.5 %collective-permute-start.1 = (bf16[64,1792]{1,0:T(8,128)(2,1)S(1)}, bf16[64,1792]{1,0:T(8,128)(2,1)S(1)}, u32[]{:S(2)}, u32[]{:S(2)}) collective-permute-start(bf16[64,1792]{1,0:T(8,128)(2,1)S(1)} %pad_maximum_fusion.2), channel_id=1, source_target_pairs={{0,32},{32,0},{1,33},{33,1},{2,34},{34,2},{3,35},{35,3},{4,36},{36... | collective-permute-start | bytes 688136 | tf_op jit(solution)/shard_map/ppermute | solution.py:124
  7.6 15.3 %collective-permute-start = (bf16[64,1792]{1,0:T(8,128)(2,1)S(1)}, bf16[64,1792]{1,0:T(8,128)(2,1)S(1)}, u32[]{:S(2)}, u32[]{:S(2)}) collective-permute-start(bf16[64,1792]{1,0:T(8,128)(2,1)S(1)} %pad_maximum_fusion.2), channel_id=1, source_target_pairs={{0,64},{1,449},{64,0},{65,129},{128,192},{129,65},{192,128},{193,2... | collective-permute-start | bytes 688136 | tf_op jit(solution)/shard_map/ppermute | solution.py:42
  15.5 24.9 %copy-start.14 = (bf16[64,512]{1,0:T(8,128)(2,1)S(1)}, bf16[64,512]{1,0:T(8,128)(2,1)}, u32[]{:S(2)}) copy-start(bf16[64,512]{1,0:T(8,128)(2,1)} %param.4) | copy-start | bytes 196612
  15.5 44.9 %collective-permute-start.2 = (bf16[512,896]{0,1:T(8,128)(2,1)}, bf16[512,896]{0,1:T(8,128)(2,1)}, u32[]{:S(2)}, u32[]{:S(2)}) collective-permute-start(bf16[512,896]{0,1:T(8,128)(2,1)} %bitcast_multiply_fusion), channel_id=1, source_target_pairs={{0,1},{1,0},{2,3},{3,2},{4,5},{5,4},{6,7},{7,6},{8,9},{9,8},{10,11... | collective-permute-start | bytes 2752520 | tf_op jit(solution)/shard_map/ppermute | solution.py:131
  22.9 18.7 %copy-start.12 = (bf16[64,1792]{1,0:T(8,128)(2,1)}, bf16[64,1792]{1,0:T(8,128)(2,1)S(1)}, u32[]{:S(2)}) copy-start(bf16[64,1792]{1,0:T(8,128)(2,1)S(1)} %collective-permute-done) | copy-start | bytes 688132
  22.9 28.7 %collective-permute-start.3 = (bf16[128,1792]{1,0:T(8,128)(2,1)S(1)}, bf16[128,1792]{1,0:T(8,128)(2,1)S(1)}, u32[]{:S(2)}, u32[]{:S(2)}) collective-permute-start(bf16[128,1792]{1,0:T(8,128)(2,1)S(1)} %pad_maximum_fusion.1.refs_0_), channel_id=1, source_target_pairs={{0,448},{1,65},{64,128},{65,1},{128,64},{129,193},{192,256},{193,1... | collective-permute-start | bytes 1376264 | tf_op jit(solution)/shard_map/ppermute | solution.py:42
  28.6 9.1 %collective-permute-start.6 = (bf16[64,1792]{1,0:T(8,128)(2,1)S(1)}, bf16[64,1792]{1,0:T(8,128)(2,1)S(1)}, u32[]{:S(2)}, u32[]{:S(2)}) collective-permute-start(bf16[64,1792]{1,0:T(8,128)(2,1)S(1)} %collective-permute-done.1), channel_id=1, source_target_pairs={{0,448},{1,65},{64,128},{65,1},{128,64},{129,193},{192,256},{193,1... | collective-permute-start | bytes 688136 | tf_op jit(solution)/shard_map/ppermute | solution.py:42
  37.8 17.8 %collective-permute-start.7 = (bf16[128,1792]{1,0:T(8,128)(2,1)S(1)}, bf16[128,1792]{1,0:T(8,128)(2,1)S(1)}, u32[]{:S(2)}, u32[]{:S(2)}) collective-permute-start(bf16[128,1792]{1,0:T(8,128)(2,1)S(1)} %constant_dynamic-update-slice_fusion.refs_4_), channel_id=1, source_target_pairs={{0,64},{1,449},{64,0},{65,129},{128,192},{129,65},{192,128},{193,2... | collective-permute-start | bytes 1376264 | tf_op jit(solution)/shard_map/ppermute | solution.py:42
  41.5 44.8 %all-to-all-start.1 = ((bf16[16,64,512]{2,1,0:T(8,128)(2,1)}), bf16[16,64,512]{2,1,0:T(8,128)(2,1)S(1)}, u32[]{:S(2)}, u32[]{:S(2)}) async-start(bf16[16,64,512]{2,1,0:T(8,128)(2,1)} %broadcast_in_dim.5), calls=%async_computation.1 | async-start | bytes 2097152 | tf_op jit(solution)/shard_map/all_to_all | solution.py:135
  51.6 14.8 %collective-permute-start.4 = (bf16[128,1792]{1,0:T(8,128)(2,1)S(1)}, bf16[128,1792]{1,0:T(8,128)(2,1)S(1)}, u32[]{:S(2)}, u32[]{:S(2)}) collective-permute-start(bf16[128,1792]{1,0:T(8,128)(2,1)S(1)} %collective-permute-done.3.refs_1_), channel_id=1, source_target_pairs={{0,64},{1,449},{64,0},{65,129},{128,192},{129,65},{192,128},{193,2... | collective-permute-start | bytes 1376264 | tf_op jit(solution)/shard_map/ppermute | solution.py:42
  55.5 17.6 %collective-permute-start.8 = (bf16[128,1792]{1,0:T(8,128)(2,1)S(1)}, bf16[128,1792]{1,0:T(8,128)(2,1)S(1)}, u32[]{:S(2)}, u32[]{:S(2)}) collective-permute-start(bf16[128,1792]{1,0:T(8,128)(2,1)S(1)} %collective-permute-done.7.refs_5_), channel_id=1, source_target_pairs={{0,448},{1,65},{64,128},{65,1},{128,64},{129,193},{192,256},{193,1... | collective-permute-start | bytes 1376264 | tf_op jit(solution)/shard_map/ppermute | solution.py:42
  66.4 16.3 %collective-permute-start.5 = (bf16[128,1792]{1,0:T(8,128)(2,1)S(1)}, bf16[128,1792]{1,0:T(8,128)(2,1)S(1)}, u32[]{:S(2)}, u32[]{:S(2)}) collective-permute-start(bf16[128,1792]{1,0:T(8,128)(2,1)S(1)} %collective-permute-done.4.refs_2_), channel_id=1, source_target_pairs={{0,448},{1,65},{64,128},{65,1},{128,64},{129,193},{192,256},{193,1... | collective-permute-start | bytes 1376264 | tf_op jit(solution)/shard_map/ppermute | solution.py:42
  71.7 0.9 copy-start.10
  71.8 1.0 copy-start.13
  73.2 10.0 %copy-start = (bf16[128,1792]{1,0:T(8,128)(2,1)}, bf16[128,1792]{1,0:T(8,128)(2,1)S(1)}, u32[]{:S(2)}) copy-start(bf16[128,1792]{1,0:T(8,128)(2,1)S(1)} %collective-permute-done.8.refs_6_) | copy-start | bytes 1376260
  73.2 10.4 %collective-permute-start.9 = (bf16[128,1792]{1,0:T(8,128)(2,1)S(1)}, bf16[128,1792]{1,0:T(8,128)(2,1)S(1)}, u32[]{:S(2)}, u32[]{:S(2)}) collective-permute-start(bf16[128,1792]{1,0:T(8,128)(2,1)S(1)} %collective-permute-done.8.refs_6_), channel_id=1, source_target_pairs={{0,64},{1,449},{64,0},{65,129},{128,192},{129,65},{192,128},{193,2... | collective-permute-start | bytes 1376264 | tf_op jit(solution)/shard_map/ppermute | solution.py:42
  82.7 0.8 copy-start.3
  84.0 0.8 copy-start.5
  86.3 36.3 %all-to-all-start = ((bf16[16,64,512]{2,1,0:T(8,128)(2,1)}), bf16[16,64,512]{2,1,0:T(8,128)(2,1)}, u32[]{:S(2)}, u32[]{:S(2)}) async-start(bf16[16,64,512]{2,1,0:T(8,128)(2,1)} %bitcast.18), calls=%async_computation | async-start | bytes 2097152 | tf_op jit(solution)/shard_map/all_to_all | solution.py:144
  95.9 1.0 copy-start.1
  97.0 1.0 copy-start.4
  98.0 1.0 copy-start.6
  99.0 6.2 %copy-start.2 = (bf16[128,1792]{1,0:T(8,128)(2,1)S(1)}, bf16[128,1792]{1,0:T(8,128)(2,1)}, u32[]{:S(2)}) copy-start(bf16[128,1792]{1,0:T(8,128)(2,1)} %copy-done) | copy-start | bytes 1376260
  99.0 6.2 %copy-start.7 = (bf16[128,1792]{1,0:T(8,128)(2,1)S(1)}, bf16[128,1792]{1,0:T(8,128)(2,1)}, u32[]{:S(2)}) copy-start(bf16[128,1792]{1,0:T(8,128)(2,1)} %copy-done.5) | copy-start | bytes 1376260
  99.0 6.2 %copy-start.8 = (s32[4,7]{1,0:T(4,128)S(1)}, s32[4,7]{1,0:T(4,128)}, u32[]{:S(2)}) copy-start(s32[4,7]{1,0:T(4,128)} %mask.1) | copy-start | bytes 340
  100.9 4.4 %collective-permute-start.10 = (bf16[512,896]{1,0:T(8,128)(2,1)S(1)}, bf16[512,896]{1,0:T(8,128)(2,1)S(1)}, u32[]{:S(2)}, u32[]{:S(2)}) collective-permute-start(bf16[512,896]{1,0:T(8,128)(2,1)S(1)} %get-tuple-element.9), channel_id=1, source_target_pairs={{0,1},{1,0},{2,3},{3,2},{4,5},{5,4},{6,7},{7,6},{8,9},{9,8},{10,11... | collective-permute-start | bytes 2752520 | tf_op jit(solution)/shard_map/ppermute | solution.py:149

commit v3 on v2

--- a/solution.py
+++ b/solution.py
@@ -68,18 +68,18 @@
 
 def place_kernel(order, *refs):
     parts, out = refs[:-1], refs[-1]
-    rows = parts[0].shape[0] // 2
+    rows = parts[0].shape[0] // 4
     for k, part in enumerate(parts):
-        for i in range(2):
-            out[block_at(order[2 * k + i], rows)] = part[i * rows : (i + 1) * rows]
+        for i in range(4):
+            out[block_at(order[4 * k + i], rows)] = part[i * rows : (i + 1) * rows]
 
 
 def away_kernel(order, quad, *refs):
     parts, in_rows, away, held = refs[:-3], refs[-3], refs[-2], refs[-1]
     rows, hidden = quad.shape[1], away.shape[1]
     for k, part in enumerate(parts):
-        held[2 * k * rows : (2 * k + 2) * rows] = part[:, hidden:]
-        for i in range(2 * k, 2 * k + 2):
+        held[4 * k * rows : (4 * k + 4) * rows] = part[:, hidden:]
+        for i in range(4 * k, 4 * k + 4):
             in_rows[i * rows : (i + 1) * rows] = quad[order[i]]
     away[...] = dot(in_rows[...], held[...], (0, 0)).astype(jnp.bfloat16)
 
@@ -109,11 +109,9 @@
     here = (z - core) % 8
     other, one = here ^ 1, next_pair(here, 8)
     two, far = next_pair(other, 8), next_pair(one ^ 1, 8)
-    ring = [here, other, one, one ^ 1, two, two ^ 1, far, far ^ 1]
-    three = two ^ 1
-    ring += [here, one, other, two, one ^ 1, next_pair(one ^ 1, 8), three, next_pair(three, 8)]
+    ring = (here, other, one, one ^ 1, two, two ^ 1, far, far ^ 1)
     spots = [(s + core) % 8 for s in ring]
-    chips = [spot // 2 * 4 + spot % 2 * 2 + (r if i < 8 else 1 - r) for i, spot in enumerate(spots)]
+    chips = [spot // 2 * 4 + spot % 2 * 2 + (r ^ i) for spot in spots for i in range(2)]
     order = jnp.stack(chips).astype(jnp.int32)
 
     both = lax.all_gather(grad_out, "core", axis=0)
@@ -121,24 +119,19 @@
     sibling = lax.dynamic_slice(both, (1 - core, core * rows, 0), (1, rows, hidden))[0]
     first = jnp.concatenate([own, sibling], axis=1)
 
-    across = lax.ppermute(first, "y_lo", SWAP)
-    a1 = swap(first, "z", near)
-    a1 = jnp.concatenate([first, a1], axis=0)
-    a2 = swap(a1, "z", next_pair)
-    b1 = swap(across, "z", next_pair)
-    b1 = jnp.concatenate([across, b1], axis=0)
-    masked = after(weight, across) * expand_mask(block_mask, side, jnp.bfloat16)
+    first = jnp.concatenate([first, lax.ppermute(first, "y_lo", SWAP)], axis=0)
+    second = swap(first, "z", near)
+    masked = after(weight, first) * expand_mask(block_mask, side, jnp.bfloat16)
     wide = jnp.concatenate([masked, lax.ppermute(masked, "core", SWAP)], axis=1)
     wide = lax.optimization_barrier(wide)
-    b2 = swap(b1, "z", near)
-    copies = jnp.broadcast_to(after(activations, a1)[None], (16,) + activations.shape)
+    pair = jnp.concatenate([first, second], axis=0)
+    third = swap(pair, "z", next_pair)
+    copies = jnp.broadcast_to(after(activations, third)[None], (16,) + activations.shape)
     quad = lax.all_to_all(copies, ("x", "y_hi"), 0, 0, tiled=True)
-    a3 = swap(a2, "z", near)
-    b3 = swap(b2, "z", next_pair)
-    a4 = swap(a3, "z", next_pair)
-    b4 = swap(b3, "z", near)
+    fourth = swap(after(third, wide), "z", near)
+    fifth = swap(fourth, "z", next_pair)
 
-    parts = (a1, a2, a3, a4, b1, b2, b3, b4)
+    parts = (pair, third, fourth, fifth)
     value = [matmul(part, wide, (1, 1)).astype(jnp.bfloat16) for part in parts]
     (value,) = call(place_kernel, [(16 * rows, width)], (order, *value), 1)
     value = lax.all_to_all(value.reshape(16, rows, width), ("x", "y_hi"), 0, 0, tiled=True)

time: 126 us -> 127 us (level)
  the two profiles are of different devices: /device:TPU:6 before, /device:TPU:17 now
where the time goes in v3:
time: 127 us; the launch traced here: 126 us
  waiting for transfers between devices  55.6 us (44%)
  starting transfers between devices  43.7 us (34%)
  Pallas kernels  8.11 us (6%)
  matrix products  6.67 us (5%)
  other arithmetic  5.44 us (4%)
  local copies, waits for them, and re-layouts  3.07 us (2%)
  blocking collectives  2.78 us (2%)
    ppermute x4, waiting for transfers between devices, swap(): return lax.ppermute(value, (axis, 'core'), pairs)  22.2 us
    ppermute x4, starting transfers between devices, swap(): return lax.ppermute(value, (axis, 'core'), pairs)  19.2 us
    all_to_all x1, waiting for transfers between devices, shards(): lax.all_to_all(value.reshape(16, rows, width), ('x', 'y_hi'), 0, 0, tiled...  17.4 us
    all_to_all x1, starting transfers between devices, shards(): quad = lax.all_to_all(copies, ('x', 'y_hi'), 0, 0, tiled=True)  9.35 us
    all_to_all x1, waiting for transfers between devices, shards(): quad = lax.all_to_all(copies, ('x', 'y_hi'), 0, 0, tiled=True)  8.37 us
    pallas_call x3, Pallas kernels, call(): pl.pallas_call(kernel, out_shape=[jax.ShapeDtypeStruct(shape, jnp.bfloat1...  8.11 us
    all_to_all x1, starting transfers between devices, shards(): lax.all_to_all(value.reshape(16, rows, width), ('x', 'y_hi'), 0, 0, tiled...  6.69 us
    dot_general x4, matrix products, matmul(): lax.dot_general(a, b, ((contract[:1], contract[1:]), ((), ())), preferred...  6.67 us
  transfers between devices with their start and end apart: 9, of which 8 were waited for; matrix products, arithmetic and copies ran while one was open for 9% of the time, Pallas kernels for 6%

profile of v3, /device:TPU:17, one launch (start us, length us, event | category | flops | bytes accessed | tf_op | source)
XLA Modules:
  0.0 126.5 jit_solution(8185427119344645405)
XLA Ops:
  0.7 2.8 %all-gather = bf16[256,896]{1,0:T(8,128)(2,1)S(1)} all-gather(bf16[128,896]{1,0:T(8,128)(2,1)} %param.5), channel_id=2, replica_groups=mesh['z'=8,'y_lo'=2,'x'=4,'y_hi'=4,'core'=2] {'core'}, dimensions={0}, use_global_device_ids=true | all-gather | bytes 688128 | tf_op jit(solution)/shard_map/all_gather | solution.py:117
  3.4 0.9 constant_dynamic-slice_fusion
  4.4 3.2 %collective-permute-start = (bf16[64,1792]{1,0:T(8,128)(2,1)S(1)}, bf16[64,1792]{1,0:T(8,128)(2,1)S(1)}, u32[]{:S(2)}, u32[]{:S(2)}) collective-permute-start(bf16[64,1792]{1,0:T(8,128)(2,1)S(1)} %pad_maximum_fusion.3), channel_id=1, source_target_pairs={{0,32},{32,0},{1,33},{33,1},{2,34},{34,2},{3,35},{35,3},{4,36},{36... | collective-permute-start | bytes 688136 | tf_op jit(solution)/shard_map/ppermute | solution.py:122
  7.6 5.5 %collective-permute-done = bf16[64,1792]{1,0:T(8,128)(2,1)S(1)} collective-permute-done((bf16[64,1792]{1,0:T(8,128)(2,1)S(1)}, bf16[64,1792]{1,0:T(8,128)(2,1)S(1)}, u32[]{:S(2)}, u32[]{:S(2)}) %collective-permute-start) | collective-permute-done | bytes 229408 | tf_op jit(solution)/shard_map/ppermute | solution.py:122
  13.1 0.8 pad_maximum_fusion.2
  13.9 10.7 %collective-permute-start.1 = (bf16[128,1792]{1,0:T(8,128)(2,1)}, bf16[128,1792]{1,0:T(8,128)(2,1)}, u32[]{:S(2)}, u32[]{:S(2)}) collective-permute-start(bf16[128,1792]{1,0:T(8,128)(2,1)} %pad_maximum_fusion.2), channel_id=1, source_target_pairs={{0,64},{1,449},{64,0},{65,129},{128,192},{129,65},{192,128},{193,2... | collective-permute-start | bytes 1376264 | tf_op jit(solution)/shard_map/ppermute | solution.py:42
  24.7 0.5 copy.7
  25.7 1.9 %collective-permute-start.2 = (bf16[512,896]{0,1:T(8,128)(2,1)S(1)}, bf16[512,896]{0,1:T(8,128)(2,1)S(1)}, u32[]{:S(2)}, u32[]{:S(2)}) collective-permute-start(bf16[512,896]{0,1:T(8,128)(2,1)S(1)} %bitcast_multiply_fusion), channel_id=1, source_target_pairs={{0,1},{1,0},{2,3},{3,2},{4,5},{5,4},{6,7},{7,6},{8,9},{9,8},{10,11... | collective-permute-start | bytes 2752520 | tf_op jit(solution)/shard_map/ppermute | solution.py:125
  27.6 3.1 %collective-permute-done.1 = bf16[128,1792]{1,0:T(8,128)(2,1)} collective-permute-done((bf16[128,1792]{1,0:T(8,128)(2,1)}, bf16[128,1792]{1,0:T(8,128)(2,1)}, u32[]{:S(2)}, u32[]{:S(2)}) %collective-permute-start.1) | collective-permute-done | bytes 458784 | tf_op jit(solution)/shard_map/ppermute | solution.py:42
  30.8 1.1 pad_maximum_fusion.1.refs_0_
  31.9 2.1 %collective-permute-start.3 = (bf16[256,1792]{1,0:T(8,128)(2,1)S(1)}, bf16[256,1792]{1,0:T(8,128)(2,1)S(1)}, u32[]{:S(2)}, u32[]{:S(2)}) collective-permute-start(bf16[256,1792]{1,0:T(8,128)(2,1)S(1)} %pad_maximum_fusion.1.refs_0_), channel_id=1, source_target_pairs={{0,448},{1,65},{64,128},{65,1},{128,64},{129,193},{192,256},{193,1... | collective-permute-start | bytes 2752520 | tf_op jit(solution)/shard_map/ppermute | solution.py:42
  33.9 1.4 %pad_maximum_fusion = bf16[512,1792]{0,1:T(8,128)(2,1)} fusion(bf16[512,896]{0,1:T(8,128)(2,1)S(1)} %collective-permute-done.2, bf16[512,896]{0,1:T(8,128)(2,1)S(1)} %bitcast_multiply_fusion), kind=kLoop, calls=%fused_computation | loop fusion | flops 3670016 | bytes 3670016 | tf_op jit(solution)/shard_map/concatenate | solution.py:125
  35.3 11.1 %collective-permute-done.3.refs_1_ = bf16[256,1792]{1,0:T(8,128)(2,1)S(1)} collective-permute-done((bf16[256,1792]{1,0:T(8,128)(2,1)S(1)}, bf16[256,1792]{1,0:T(8,128)(2,1)S(1)}, u32[]{:S(2)}, u32[]{:S(2)}) %collective-permute-start.3) | collective-permute-done | bytes 917536 | tf_op jit(solution)/shard_map/ppermute | solution.py:42
  46.4 4.6 %collective-permute-start.4 = (bf16[256,1792]{1,0:T(8,128)(2,1)S(1)}, bf16[256,1792]{1,0:T(8,128)(2,1)}, u32[]{:S(2)}, u32[]{:S(2)}) collective-permute-start(bf16[256,1792]{1,0:T(8,128)(2,1)S(1)} %collective-permute-done.3.refs_1_), channel_id=1, source_target_pairs={{0,64},{1,449},{64,0},{65,129},{128,192},{129,65},{192,128},{193,2... | collective-permute-start | bytes 2752520 | tf_op jit(solution)/shard_map/ppermute | solution.py:42
  51.0 1.1 broadcast_in_dim.5
  52.1 9.3 %all-to-all-start.1 = ((bf16[16,64,512]{2,1,0:T(8,128)(2,1)}), bf16[16,64,512]{2,1,0:T(8,128)(2,1)S(1)}, u32[]{:S(2)}, u32[]{:S(2)}) async-start(bf16[16,64,512]{2,1,0:T(8,128)(2,1)} %broadcast_in_dim.5), calls=%async_computation.1 | async-start | bytes 2097152 | tf_op jit(solution)/shard_map/all_to_all | solution.py:130
  61.4 0.4 collective-permute-done.4.refs_2_
  61.9 1.9 %collective-permute-start.5 = (bf16[256,1792]{1,0:T(8,128)(2,1)}, bf16[256,1792]{1,0:T(8,128)(2,1)}, u32[]{:S(2)}, u32[]{:S(2)}) collective-permute-start(bf16[256,1792]{1,0:T(8,128)(2,1)} %collective-permute-done.4.refs_2_), channel_id=1, source_target_pairs={{0,448},{1,65},{64,128},{65,1},{128,64},{129,193},{192,256},{193,1... | collective-permute-start | bytes 2752520 | tf_op jit(solution)/shard_map/ppermute | solution.py:42
  64.2 2.4 %convolution_convert_fusion.3.refs_0_ = bf16[256,512]{1,0:T(8,128)(2,1)S(1)} fusion(bf16[512,1792]{0,1:T(8,128)(2,1)} %pad_maximum_fusion, bf16[128,1792]{1,0:T(8,128)(2,1)} %collective-permute-done.1, bf16[64,1792]{1,0:T(8,128)(2,1)S(1)} %collective-permute-done, bf16[64,896]{1,0:T(8,128)(2,1)S(1)} %dynamic-slice_bitcast_fusion, ...), kind=kOutput, calls=%fused_computation.4 | convolution fusion | flops 473563136 | bytes 3014656 | tf_op jit(solution)/shard_map/dot_general | solution.py:24
  66.6 0.6 convolution_convert_fusion.2.refs_1_
  67.2 1.8 %convolution_convert_fusion.1.refs_2_ = bf16[256,512]{1,0:T(8,128)(2,1)S(1)} fusion(bf16[256,1792]{1,0:T(8,128)(2,1)} %collective-permute-done.4.refs_2_, bf16[512,1792]{0,1:T(8,128)(2,1)S(1)} %copy-done.1), kind=kOutput, calls=%fused_computation.2 | convolution fusion | flops 469893120 | bytes 3014656 | tf_op jit(solution)/shard_map/dot_general | solution.py:24
  69.0 7.6 %collective-permute-done.5.refs_3_ = bf16[256,1792]{1,0:T(8,128)(2,1)} collective-permute-done((bf16[256,1792]{1,0:T(8,128)(2,1)}, bf16[256,1792]{1,0:T(8,128)(2,1)}, u32[]{:S(2)}, u32[]{:S(2)}) %collective-permute-start.5) | collective-permute-done | bytes 917536 | tf_op jit(solution)/shard_map/ppermute | solution.py:42
  76.6 1.8 %convolution_convert_fusion.refs_3_ = bf16[256,512]{1,0:T(8,128)(2,1)S(1)} fusion(bf16[256,1792]{1,0:T(8,128)(2,1)} %collective-permute-done.5.refs_3_, bf16[512,1792]{0,1:T(8,128)(2,1)S(1)} %copy-done.1), kind=kOutput, calls=%fused_computation.1 | convolution fusion | flops 469893120 | bytes 3014656 | tf_op jit(solution)/shard_map/dot_general | solution.py:24
  78.4 1.6 %shard_map.59 = bf16[1024,512]{1,0:T(8,128)(2,1)} custom-call(s32[16]{0:T(128)S(1)} %stack.67.order, bf16[256,512]{1,0:T(8,128)(2,1)S(1)} %convolution_convert_fusion.3.refs_0_, bf16[256,512]{1,0:T(8,128)(2,1)S(1)} %convolution_convert_fusion.2.refs_1_, bf16[256,512]{1,0:T(8,128)(2,1)S(1)} %convolution_convert_fusion.1.refs_2_, ...), custom_call_target="tpu_custom_call" | custom-call | tf_op jit(solution)/shard_map/pallas_call | solution.py:51
  80.0 8.4 %all-to-all-done.1.quad = bf16[16,64,512]{2,1,0:T(8,128)(2,1)S(1)} async-done(((bf16[16,64,512]{2,1,0:T(8,128)(2,1)}), bf16[16,64,512]{2,1,0:T(8,128)(2,1)S(1)}, u32[]{:S(2)}, u32[]{:S(2)}) %all-to-all-start.1) | async-done | bytes 1048608 | tf_op jit(solution)/shard_map/all_to_all | solution.py:130
  88.4 6.7 %all-to-all-start = ((bf16[16,64,512]{2,1,0:T(8,128)(2,1)}), bf16[16,64,512]{2,1,0:T(8,128)(2,1)}, u32[]{:S(2)}, u32[]{:S(2)}) async-start(bf16[16,64,512]{2,1,0:T(8,128)(2,1)} %bitcast.18), calls=%async_computation | async-start | bytes 2097152 | tf_op jit(solution)/shard_map/all_to_all | solution.py:137
  95.1 2.8 %shard_map.60 = (bf16[1024,512]{1,0:T(8,128)(2,1)S(1)}, bf16[512,896]{1,0:T(8,128)(2,1)S(1)}) custom-call(s32[16]{0:T(128)S(1)} %stack.67.order, bf16[16,64,512]{2,1,0:T(8,128)(2,1)S(1)} %all-to-all-done.1.quad, bf16[256,1792]{1,0:T(8,128)(2,1)S(1)} %pad_maximum_fusion.1.refs_0_, bf16[256,1792]{1,0:T(8,128)(2,1)S(1)} %collective-permute-done.3.refs_1_, ...), custom_call_target="tpu_custom_call" | custom-call | tf_op jit(solution)/shard_map/pallas_call | solution.py:51
  97.9 3.4 %collective-permute-start.6 = (bf16[512,896]{1,0:T(8,128)(2,1)S(1)}, bf16[512,896]{1,0:T(8,128)(2,1)S(1)}, u32[]{:S(2)}, u32[]{:S(2)}) collective-permute-start(bf16[512,896]{1,0:T(8,128)(2,1)S(1)} %get-tuple-element.11), channel_id=1, source_target_pairs={{0,1},{1,0},{2,3},{3,2},{4,5},{5,4},{6,7},{7,6},{8,9},{9,8},{10,11... | collective-permute-start | bytes 2752520 | tf_op jit(solution)/shard_map/ppermute | solution.py:142
  101.3 2.1 %collective-permute-done.6.received = bf16[512,896]{1,0:T(8,128)(2,1)S(1)} collective-permute-done((bf16[512,896]{1,0:T(8,128)(2,1)S(1)}, bf16[512,896]{1,0:T(8,128)(2,1)S(1)}, u32[]{:S(2)}, u32[]{:S(2)}) %collective-permute-start.6) | collective-permute-done | bytes 917536 | tf_op jit(solution)/shard_map/ppermute | solution.py:142
  103.3 3.7 %shard_map.61 = bf16[512,896]{1,0:T(8,128)(2,1)} custom-call(s32[4,7]{1,0:T(4,128)S(1)} %copy-done, bf16[1024,512]{1,0:T(8,128)(2,1)S(1)} %get-tuple-element.10.in_rows, bf16[512,896]{1,0:T(8,128)(2,1)S(1)} %collective-permute-done.6.received, bf16[256,1792]{1,0:T(8,128)(2,1)S(1)} %pad_maximum_fusion.1.refs_0_, ...), custom_call_target="tpu_custom_call" | custom-call | tf_op jit(solution)/shard_map/pallas_call | solution.py:51
  107.1 17.4 %all-to-all-done = bf16[16,64,512]{2,1,0:T(8,128)(2,1)} async-done(((bf16[16,64,512]{2,1,0:T(8,128)(2,1)}), bf16[16,64,512]{2,1,0:T(8,128)(2,1)}, u32[]{:S(2)}, u32[]{:S(2)}) %all-to-all-start) | async-done | bytes 1048608 | tf_op jit(solution)/shard_map/all_to_all | solution.py:137
  124.5 2.0 %reduce_sum.12 = bf16[64,512]{1,0:T(8,128)(2,1)} reduce(bf16[16,64,512]{2,1,0:T(8,128)(2,1)} %all-to-all-done, bf16[]{:T(256)} %constant.231.clone.1), dimensions={0}, to_apply=%region_0.1 | reduce | flops 491520 | bytes 1114114 | tf_op jit(solution)/shard_map/reduce_sum | solution.py:138
  (16 shorter events, 0.7 us)
Async XLA Ops:
  0.6 24.0 %copy-start = (s32[4,7]{1,0:T(4,128)S(1)}, s32[4,7]{1,0:T(4,128)}, u32[]{:S(2)}) copy-start(s32[4,7]{1,0:T(4,128)} %mask.1) | copy-start | bytes 340
  0.6 24.1 %copy-start.2 = (bf16[512,896]{1,0:T(8,128)(2,1)S(1)}, bf16[512,896]{1,0:T(8,128)(2,1)}, u32[]{:S(2)}) copy-start(bf16[512,896]{1,0:T(8,128)(2,1)} %param.6) | copy-start | bytes 2752516
  4.4 8.7 %collective-permute-start = (bf16[64,1792]{1,0:T(8,128)(2,1)S(1)}, bf16[64,1792]{1,0:T(8,128)(2,1)S(1)}, u32[]{:S(2)}, u32[]{:S(2)}) collective-permute-start(bf16[64,1792]{1,0:T(8,128)(2,1)S(1)} %pad_maximum_fusion.3), channel_id=1, source_target_pairs={{0,32},{32,0},{1,33},{33,1},{2,34},{34,2},{3,35},{35,3},{4,36},{36... | collective-permute-start | bytes 688136 | tf_op jit(solution)/shard_map/ppermute | solution.py:122
  13.9 16.8 %collective-permute-start.1 = (bf16[128,1792]{1,0:T(8,128)(2,1)}, bf16[128,1792]{1,0:T(8,128)(2,1)}, u32[]{:S(2)}, u32[]{:S(2)}) collective-permute-start(bf16[128,1792]{1,0:T(8,128)(2,1)} %pad_maximum_fusion.2), channel_id=1, source_target_pairs={{0,64},{1,449},{64,0},{65,129},{128,192},{129,65},{192,128},{193,2... | collective-permute-start | bytes 1376264 | tf_op jit(solution)/shard_map/ppermute | solution.py:42
  25.7 8.2 %collective-permute-start.2 = (bf16[512,896]{0,1:T(8,128)(2,1)S(1)}, bf16[512,896]{0,1:T(8,128)(2,1)S(1)}, u32[]{:S(2)}, u32[]{:S(2)}) collective-permute-start(bf16[512,896]{0,1:T(8,128)(2,1)S(1)} %bitcast_multiply_fusion), channel_id=1, source_target_pairs={{0,1},{1,0},{2,3},{3,2},{4,5},{5,4},{6,7},{7,6},{8,9},{9,8},{10,11... | collective-permute-start | bytes 2752520 | tf_op jit(solution)/shard_map/ppermute | solution.py:125
  31.8 19.1 %copy-start.3 = (bf16[64,512]{1,0:T(8,128)(2,1)S(1)}, bf16[64,512]{1,0:T(8,128)(2,1)}, u32[]{:S(2)}) copy-start(bf16[64,512]{1,0:T(8,128)(2,1)} %param.4) | copy-start | bytes 196612
  31.9 14.6 %collective-permute-start.3 = (bf16[256,1792]{1,0:T(8,128)(2,1)S(1)}, bf16[256,1792]{1,0:T(8,128)(2,1)S(1)}, u32[]{:S(2)}, u32[]{:S(2)}) collective-permute-start(bf16[256,1792]{1,0:T(8,128)(2,1)S(1)} %pad_maximum_fusion.1.refs_0_), channel_id=1, source_target_pairs={{0,448},{1,65},{64,128},{65,1},{128,64},{129,193},{192,256},{193,1... | collective-permute-start | bytes 2752520 | tf_op jit(solution)/shard_map/ppermute | solution.py:42
  46.4 15.4 %collective-permute-start.4 = (bf16[256,1792]{1,0:T(8,128)(2,1)S(1)}, bf16[256,1792]{1,0:T(8,128)(2,1)}, u32[]{:S(2)}, u32[]{:S(2)}) collective-permute-start(bf16[256,1792]{1,0:T(8,128)(2,1)S(1)} %collective-permute-done.3.refs_1_), channel_id=1, source_target_pairs={{0,64},{1,449},{64,0},{65,129},{128,192},{129,65},{192,128},{193,2... | collective-permute-start | bytes 2752520 | tf_op jit(solution)/shard_map/ppermute | solution.py:42
  52.1 36.3 %all-to-all-start.1 = ((bf16[16,64,512]{2,1,0:T(8,128)(2,1)}), bf16[16,64,512]{2,1,0:T(8,128)(2,1)S(1)}, u32[]{:S(2)}, u32[]{:S(2)}) async-start(bf16[16,64,512]{2,1,0:T(8,128)(2,1)} %broadcast_in_dim.5), calls=%async_computation.1 | async-start | bytes 2097152 | tf_op jit(solution)/shard_map/all_to_all | solution.py:130
  61.9 14.7 %collective-permute-start.5 = (bf16[256,1792]{1,0:T(8,128)(2,1)}, bf16[256,1792]{1,0:T(8,128)(2,1)}, u32[]{:S(2)}, u32[]{:S(2)}) collective-permute-start(bf16[256,1792]{1,0:T(8,128)(2,1)} %collective-permute-done.4.refs_2_), channel_id=1, source_target_pairs={{0,448},{1,65},{64,128},{65,1},{128,64},{129,193},{192,256},{193,1... | collective-permute-start | bytes 2752520 | tf_op jit(solution)/shard_map/ppermute | solution.py:42
  64.1 2.4 %copy-start.1 = (bf16[512,1792]{0,1:T(8,128)(2,1)S(1)}, bf16[512,1792]{0,1:T(8,128)(2,1)}, u32[]{:S(2)}) copy-start(bf16[512,1792]{0,1:T(8,128)(2,1)} %pad_maximum_fusion) | copy-start | bytes 5505028
  88.4 36.1 %all-to-all-start = ((bf16[16,64,512]{2,1,0:T(8,128)(2,1)}), bf16[16,64,512]{2,1,0:T(8,128)(2,1)}, u32[]{:S(2)}, u32[]{:S(2)}) async-start(bf16[16,64,512]{2,1,0:T(8,128)(2,1)} %bitcast.18), calls=%async_computation | async-start | bytes 2097152 | tf_op jit(solution)/shard_map/all_to_all | solution.py:137
  97.9 5.5 %collective-permute-start.6 = (bf16[512,896]{1,0:T(8,128)(2,1)S(1)}, bf16[512,896]{1,0:T(8,128)(2,1)S(1)}, u32[]{:S(2)}, u32[]{:S(2)}) collective-permute-start(bf16[512,896]{1,0:T(8,128)(2,1)S(1)} %get-tuple-element.11), channel_id=1, source_target_pairs={{0,1},{1,0},{2,3},{3,2},{4,5},{5,4},{6,7},{7,6},{8,9},{9,8},{10,11... | collective-permute-start | bytes 2752520 | tf_op jit(solution)/shard_map/ppermute | solution.py:142

commit v4 on v2

--- a/solution.py
+++ b/solution.py
@@ -40,6 +40,11 @@
             there = (partner((place - core) % size, size) + core) % size
             pairs.append((place * 2 + core, there * 2 + core))
     return lax.ppermute(value, (axis, "core"), pairs)
+
+
+def all_copies(value, axis):
+    copies = jnp.broadcast_to(value[None], (lax.axis_size(axis),) + value.shape)
+    return lax.all_to_all(copies, axis, 0, 0, tiled=True).reshape((-1,) + value.shape[1:])
 
 
 def after(value, *done):
@@ -109,11 +114,8 @@
     here = (z - core) % 8
     other, one = here ^ 1, next_pair(here, 8)
     two, far = next_pair(other, 8), next_pair(one ^ 1, 8)
-    ring = [here, other, one, one ^ 1, two, two ^ 1, far, far ^ 1]
-    three = two ^ 1
-    ring += [here, one, other, two, one ^ 1, next_pair(one ^ 1, 8), three, next_pair(three, 8)]
-    spots = [(s + core) % 8 for s in ring]
-    chips = [spot // 2 * 4 + spot % 2 * 2 + (r if i < 8 else 1 - r) for i, spot in enumerate(spots)]
+    spots = [(s + core) % 8 for s in (here, other, one, one ^ 1, two, two ^ 1, far, far ^ 1)]
+    chips = [spot // 2 * 4 + spot % 2 * 2 + half for half in (r, 1 - r) for spot in spots]
     order = jnp.stack(chips).astype(jnp.int32)
 
     both = lax.all_gather(grad_out, "core", axis=0)
@@ -121,35 +123,33 @@
     sibling = lax.dynamic_slice(both, (1 - core, core * rows, 0), (1, rows, hidden))[0]
     first = jnp.concatenate([own, sibling], axis=1)
 
-    across = lax.ppermute(first, "y_lo", SWAP)
+    b0 = lax.ppermute(first, "y_lo", SWAP)
     a1 = swap(first, "z", near)
-    a1 = jnp.concatenate([first, a1], axis=0)
-    a2 = swap(a1, "z", next_pair)
-    b1 = swap(across, "z", next_pair)
-    b1 = jnp.concatenate([across, b1], axis=0)
-    masked = after(weight, across) * expand_mask(block_mask, side, jnp.bfloat16)
+    line = all_copies(after(activations, first), "y_hi")
+    pair = jnp.concatenate([first, a1], axis=0)
+    a2 = swap(pair, "z", next_pair)
+    b1 = lax.ppermute(a1, "y_lo", SWAP)
+    masked = after(weight, a1) * expand_mask(block_mask, side, jnp.bfloat16)
     wide = jnp.concatenate([masked, lax.ppermute(masked, "core", SWAP)], axis=1)
     wide = lax.optimization_barrier(wide)
-    b2 = swap(b1, "z", near)
-    copies = jnp.broadcast_to(after(activations, a1)[None], (16,) + activations.shape)
-    quad = lax.all_to_all(copies, ("x", "y_hi"), 0, 0, tiled=True)
+    b2 = lax.ppermute(a2, "y_lo", SWAP)
     a3 = swap(a2, "z", near)
-    b3 = swap(b2, "z", next_pair)
+    quad = all_copies(after(line, a2, b1), "x").reshape(16, rows, width)
+    b3 = swap(after(b2, wide), "z", near)
     a4 = swap(a3, "z", next_pair)
-    b4 = swap(b3, "z", near)
+    b4 = swap(b3, "z", next_pair)
 
-    parts = (a1, a2, a3, a4, b1, b2, b3, b4)
+    parts = (pair, a2, a3, a4, jnp.concatenate([b0, b1], axis=0), b2, b3, b4)
     value = [matmul(part, wide, (1, 1)).astype(jnp.bfloat16) for part in parts]
     (value,) = call(place_kernel, [(16 * rows, width)], (order, *value), 1)
     value = lax.all_to_all(value.reshape(16, rows, width), ("x", "y_hi"), 0, 0, tiled=True)
-    grad_input = jnp.sum(value.astype(jnp.float32), axis=0).astype(jnp.bfloat16)
-
     scratch = [pltpu.VMEM((16 * rows, hidden), jnp.bfloat16)]
     in_rows, away = call(away_kernel, [(16 * rows, width), (width, hidden)], (order, quad, *parts), 1, scratch)
     received = lax.ppermute(away, "core", SWAP)
     factor = 1.0 / math.sqrt(rows * 32)
     home = functools.partial(home_kernel, factor)
     (grad_weight,) = call(home, [(width, hidden)], (block_mask, in_rows, received, *parts), 1, scratch)
+    grad_input = jnp.sum(after(value, grad_weight).astype(jnp.float32), axis=0).astype(jnp.bfloat16)
     return (grad_input, grad_weight)
 
 

time: 126 us -> 121 us (0.960)
  waiting for transfers between devices: 36.7 us -> 33.1 us
    ppermute x8 -> x6, starting transfers between devices: 29.4 us -> 19.1 us  [swap(): return lax.ppermute(value, (axis, 'core'), pairs)]
    ppermute x1 -> x3, starting transfers between devices: 3.48 us -> 9.33 us  [the longest x1 3.48 us: shards(): b0 = lax.ppermute(first, 'y_lo', SWAP)]
    ppermute x1 -> x3, waiting for transfers between devices: 0.96 us -> 5.83 us  [the longest x1 5.82 us: shards(): b1 = lax.ppermute(a1, 'y_lo', SWAP)]
    ppermute x8 -> x6, waiting for transfers between devices: 18.7 us -> 14 us  [swap(): return lax.ppermute(value, (axis, 'core'), pairs)]
    all_to_all x1, waiting for transfers between devices: 14.5 us -> 10.8 us  [shards(): lax.all_to_all(value.reshape(16, rows, width), ('x', 'y_hi'), 0, 0, tiled...]
    all_to_all x1 -> x2, starting transfers between devices: 10.1 us -> 11.9 us  [all_copies(): lax.all_to_all(copies, axis, 0, 0, tiled=True)]
  transfers between devices with their start and end apart: 13 -> 14, of which waited for: 7 -> 7; matrix products, arithmetic and copies ran while one was open for 7% -> 8% of each run, Pallas kernels for 5% -> 5%
where the time goes in v4:
time: 121 us; the launch traced here: 120 us
  starting transfers between devices  61 us (50%)
  waiting for transfers between devices  33.1 us (27%)
  local copies, waits for them, and re-layouts  7.66 us (6%)
  Pallas kernels  6.29 us (5%)
  other arithmetic  5.4 us (4%)
  matrix products  3.25 us (3%)
  blocking collectives  2.48 us (2%)
    ppermute x6, starting transfers between devices, swap(): return lax.ppermute(value, (axis, 'core'), pairs)  19.1 us
    ppermute x6, waiting for transfers between devices, swap(): return lax.ppermute(value, (axis, 'core'), pairs)  14 us
    all_to_all x2, starting transfers between devices, all_copies(): lax.all_to_all(copies, axis, 0, 0, tiled=True)  11.9 us
    all_to_all x1, waiting for transfers between devices, shards(): lax.all_to_all(value.reshape(16, rows, width), ('x', 'y_hi'), 0, 0, tiled...  10.8 us
    all_to_all x1, starting transfers between devices, shards(): lax.all_to_all(value.reshape(16, rows, width), ('x', 'y_hi'), 0, 0, tiled...  10.6 us
    ppermute x1, starting transfers between devices, shards(): wide = jnp.concatenate([masked, lax.ppermute(masked, 'core', SWAP)], axis=1)  8.14 us
    pallas_call x3, Pallas kernels, call(): pl.pallas_call(kernel, out_shape=[jax.ShapeDtypeStruct(shape, jnp.bfloat1...  6.29 us
    ppermute x1, waiting for transfers between devices, shards(): b1 = lax.ppermute(a1, 'y_lo', SWAP)  5.82 us
  transfers between devices with their start and end apart: 14, of which 7 were waited for; matrix products, arithmetic and copies ran while one was open for 8% of the time, Pallas kernels for 5%

profile of v4, /device:TPU:6, one launch (start us, length us, event | category | flops | bytes accessed | tf_op | source)
XLA Modules:
  0.0 120.2 jit_solution(7871943665143476028)
XLA Ops:
  0.6 2.5 %all-gather = bf16[256,896]{1,0:T(8,128)(2,1)S(1)} all-gather(bf16[128,896]{1,0:T(8,128)(2,1)} %param.5), channel_id=2, replica_groups=mesh['z'=8,'y_lo'=2,'x'=4,'y_hi'=4,'core'=2] {'core'}, dimensions={0}, use_global_device_ids=true | all-gather | bytes 688128 | tf_op jit(solution)/shard_map/all_gather | solution.py:121
  4.1 4.3 %collective-permute-start = (bf16[64,1792]{1,0:T(8,128)(2,1)S(1)}, bf16[64,1792]{1,0:T(8,128)(2,1)S(1)}, u32[]{:S(2)}, u32[]{:S(2)}) collective-permute-start(bf16[64,1792]{1,0:T(8,128)(2,1)S(1)} %pad_maximum_fusion.2), channel_id=1, source_target_pairs={{0,64},{1,449},{64,0},{65,129},{128,192},{129,65},{192,128},{193,2... | collective-permute-start | bytes 688136 | tf_op jit(solution)/shard_map/ppermute | solution.py:42
  8.4 3.5 %collective-permute-start.5 = (bf16[64,1792]{1,0:T(8,128)(2,1)S(1)}, bf16[64,1792]{1,0:T(8,128)(2,1)S(1)}, u32[]{:S(2)}, u32[]{:S(2)}) collective-permute-start(bf16[64,1792]{1,0:T(8,128)(2,1)S(1)} %pad_maximum_fusion.2), channel_id=1, source_target_pairs={{0,32},{32,0},{1,33},{33,1},{2,34},{34,2},{3,35},{35,3},{4,36},{36... | collective-permute-start | bytes 688136 | tf_op jit(solution)/shard_map/ppermute | solution.py:126
  13.6 1.1 bitcast_multiply_fusion
  14.6 8.1 %collective-permute-start.1 = (bf16[512,896]{0,1:T(8,128)(2,1)}, bf16[512,896]{0,1:T(8,128)(2,1)}, u32[]{:S(2)}, u32[]{:S(2)}) collective-permute-start(bf16[512,896]{0,1:T(8,128)(2,1)} %bitcast_multiply_fusion), channel_id=1, source_target_pairs={{0,1},{1,0},{2,3},{3,2},{4,5},{5,4},{6,7},{7,6},{8,9},{9,8},{10,11... | collective-permute-start | bytes 2752520 | tf_op jit(solution)/shard_map/ppermute | solution.py:133
  22.8 4.2 %collective-permute-start.2 = (bf16[128,1792]{1,0:T(8,128)(2,1)S(1)}, bf16[128,1792]{1,0:T(8,128)(2,1)S(1)}, u32[]{:S(2)}, u32[]{:S(2)}) collective-permute-start(bf16[128,1792]{1,0:T(8,128)(2,1)S(1)} %pad_maximum_fusion.1.refs_0_), channel_id=1, source_target_pairs={{0,448},{1,65},{64,128},{65,1},{128,64},{129,193},{192,256},{193,1... | collective-permute-start | bytes 1376264 | tf_op jit(solution)/shard_map/ppermute | solution.py:42
  27.8 7.1 %all-to-all-start.1 = ((bf16[4,64,512]{2,1,0:T(8,128)(2,1)}), bf16[4,64,512]{2,1,0:T(8,128)(2,1)S(1)}, u32[]{:S(2)}, u32[]{:S(2)}) async-start(bf16[4,64,512]{2,1,0:T(8,128)(2,1)} %broadcast_in_dim.7), calls=%async_computation.1 | async-start | bytes 524288 | tf_op jit(solution)/shard_map/all_to_all | solution.py:47
  35.0 2.6 %collective-permute-start.6 = (bf16[64,1792]{1,0:T(8,128)(2,1)S(1)}, bf16[64,1792]{1,0:T(8,128)(2,1)S(1)}, u32[]{:S(2)}, u32[]{:S(2)}) collective-permute-start(bf16[64,1792]{1,0:T(8,128)(2,1)S(1)} %collective-permute-done), channel_id=1, source_target_pairs={{0,32},{32,0},{1,33},{33,1},{2,34},{34,2},{3,35},{35,3},{4,36},{36... | collective-permute-start | bytes 688136 | tf_op jit(solution)/shard_map/ppermute | solution.py:131
  37.6 3.3 %collective-permute-start.7 = (bf16[128,1792]{1,0:T(8,128)(2,1)S(1)}, bf16[128,1792]{1,0:T(8,128)(2,1)S(1)}, u32[]{:S(2)}, u32[]{:S(2)}) collective-permute-start(bf16[128,1792]{1,0:T(8,128)(2,1)S(1)} %collective-permute-done.2.refs_1_), channel_id=1, source_target_pairs={{0,32},{32,0},{1,33},{33,1},{2,34},{34,2},{3,35},{35,3},{4,36},{36... | collective-permute-start | bytes 1376264 | tf_op jit(solution)/shard_map/ppermute | solution.py:135
  40.9 5.8 %collective-permute-done.6 = bf16[64,1792]{1,0:T(8,128)(2,1)S(1)} collective-permute-done((bf16[64,1792]{1,0:T(8,128)(2,1)S(1)}, bf16[64,1792]{1,0:T(8,128)(2,1)S(1)}, u32[]{:S(2)}, u32[]{:S(2)}) %collective-permute-start.6) | collective-permute-done | bytes 229408 | tf_op jit(solution)/shard_map/ppermute | solution.py:131
  46.7 1.1 broadcast_in_dim.8
  47.8 4.8 %all-to-all-start.2 = ((bf16[4,256,512]{2,1,0:T(8,128)(2,1)}), bf16[4,256,512]{2,1,0:T(8,128)(2,1)S(1)}, u32[]{:S(2)}, u32[]{:S(2)}) async-start(bf16[4,256,512]{2,1,0:T(8,128)(2,1)} %broadcast_in_dim.8), calls=%async_computation.2 | async-start | bytes 2097152 | tf_op jit(solution)/shard_map/all_to_all | solution.py:47
  52.6 1.9 %collective-permute-start.3 = (bf16[128,1792]{1,0:T(8,128)(2,1)S(1)}, bf16[128,1792]{1,0:T(8,128)(2,1)S(1)}, u32[]{:S(2)}, u32[]{:S(2)}) collective-permute-start(bf16[128,1792]{1,0:T(8,128)(2,1)S(1)} %collective-permute-done.2.refs_1_), channel_id=1, source_target_pairs={{0,64},{1,449},{64,0},{65,129},{128,192},{129,65},{192,128},{193,2... | collective-permute-start | bytes 1376264 | tf_op jit(solution)/shard_map/ppermute | solution.py:42
  54.5 1.6 %pad_maximum_fusion = bf16[512,1792]{0,1:T(8,128)(2,1)S(1)} fusion(bf16[512,896]{0,1:T(8,128)(2,1)} %collective-permute-done.1, bf16[512,896]{0,1:T(8,128)(2,1)} %bitcast_multiply_fusion), kind=kLoop, calls=%fused_computation | loop fusion | flops 3670016 | bytes 3670016 | tf_op jit(solution)/shard_map/concatenate | solution.py:133
  56.1 3.9 %collective-permute-start.8 = (bf16[128,1792]{1,0:T(8,128)(2,1)S(1)}, bf16[128,1792]{1,0:T(8,128)(2,1)S(1)}, u32[]{:S(2)}, u32[]{:S(2)}) collective-permute-start(bf16[128,1792]{1,0:T(8,128)(2,1)S(1)} %collective-permute-done.7.refs_5_), channel_id=1, source_target_pairs={{0,64},{1,449},{64,0},{65,129},{128,192},{129,65},{192,128},{193,2... | collective-permute-start | bytes 1376264 | tf_op jit(solution)/shard_map/ppermute | solution.py:42
  60.9 2.1 %collective-permute-done.3.refs_2_ = bf16[128,1792]{1,0:T(8,128)(2,1)S(1)} collective-permute-done((bf16[128,1792]{1,0:T(8,128)(2,1)S(1)}, bf16[128,1792]{1,0:T(8,128)(2,1)S(1)}, u32[]{:S(2)}, u32[]{:S(2)}) %collective-permute-start.3) | collective-permute-done | bytes 458784 | tf_op jit(solution)/shard_map/ppermute | solution.py:42
  63.4 2.9 %collective-permute-start.4 = (bf16[128,1792]{1,0:T(8,128)(2,1)S(1)}, bf16[128,1792]{1,0:T(8,128)(2,1)S(1)}, u32[]{:S(2)}, u32[]{:S(2)}) collective-permute-start(bf16[128,1792]{1,0:T(8,128)(2,1)S(1)} %collective-permute-done.3.refs_2_), channel_id=1, source_target_pairs={{0,448},{1,65},{64,128},{65,1},{128,64},{129,193},{192,256},{193,1... | collective-permute-start | bytes 1376264 | tf_op jit(solution)/shard_map/ppermute | solution.py:42
  67.1 3.1 %collective-permute-done.8.refs_6_ = bf16[128,1792]{1,0:T(8,128)(2,1)S(1)} collective-permute-done((bf16[128,1792]{1,0:T(8,128)(2,1)S(1)}, bf16[128,1792]{1,0:T(8,128)(2,1)S(1)}, u32[]{:S(2)}, u32[]{:S(2)}) %collective-permute-start.8) | collective-permute-done | bytes 458784 | tf_op jit(solution)/shard_map/ppermute | solution.py:42
  70.2 1.9 %collective-permute-start.9 = (bf16[128,1792]{1,0:T(8,128)(2,1)S(1)}, bf16[128,1792]{1,0:T(8,128)(2,1)S(1)}, u32[]{:S(2)}, u32[]{:S(2)}) collective-permute-start(bf16[128,1792]{1,0:T(8,128)(2,1)S(1)} %collective-permute-done.8.refs_6_), channel_id=1, source_target_pairs={{0,448},{1,65},{64,128},{65,1},{128,64},{129,193},{192,256},{193,1... | collective-permute-start | bytes 1376264 | tf_op jit(solution)/shard_map/ppermute | solution.py:42
  72.5 2.4 %collective-permute-done.4.refs_3_ = bf16[128,1792]{1,0:T(8,128)(2,1)S(1)} collective-permute-done((bf16[128,1792]{1,0:T(8,128)(2,1)S(1)}, bf16[128,1792]{1,0:T(8,128)(2,1)S(1)}, u32[]{:S(2)}, u32[]{:S(2)}) %collective-permute-start.4) | collective-permute-done | bytes 458784 | tf_op jit(solution)/shard_map/ppermute | solution.py:42
  75.4 6.4 %collective-permute-done.9.refs_7_ = bf16[128,1792]{1,0:T(8,128)(2,1)S(1)} collective-permute-done((bf16[128,1792]{1,0:T(8,128)(2,1)S(1)}, bf16[128,1792]{1,0:T(8,128)(2,1)S(1)}, u32[]{:S(2)}, u32[]{:S(2)}) %collective-permute-start.9) | collective-permute-done | bytes 458784 | tf_op jit(solution)/shard_map/ppermute | solution.py:42
  83.0 1.6 %shard_map.59 = bf16[1024,512]{1,0:T(8,128)(2,1)} custom-call(s32[16]{0:T(128)S(1)} %stack.67.order, bf16[128,512]{1,0:T(8,128)(2,1)S(1)} %convolution_convert_fusion.7.refs_0_, bf16[128,512]{1,0:T(8,128)(2,1)S(1)} %convolution_convert_fusion.6.refs_1_, bf16[128,512]{1,0:T(8,128)(2,1)S(1)} %convolution_convert_fusion.5.refs_2_, ...), custom_call_target="tpu_custom_call" | custom-call | tf_op jit(solution)/shard_map/pallas_call | solution.py:56
  84.6 10.6 %all-to-all-start = ((bf16[16,64,512]{2,1,0:T(8,128)(2,1)}), bf16[16,64,512]{2,1,0:T(8,128)(2,1)}, u32[]{:S(2)}, u32[]{:S(2)}) async-start(bf16[16,64,512]{2,1,0:T(8,128)(2,1)} %bitcast.18), calls=%async_computation | async-start | bytes 2097152 | tf_op jit(solution)/shard_map/all_to_all | solution.py:145
  95.2 1.0 copy-done.1
  96.2 1.0 copy-done.4
  97.2 1.0 copy-done.6
  98.2 1.9 %shard_map.60 = (bf16[1024,512]{1,0:T(8,128)(2,1)S(1)}, bf16[512,896]{1,0:T(8,128)(2,1)S(1)}) custom-call(s32[16]{0:T(128)S(1)} %stack.67.order, bf16[16,64,512]{2,1,0:T(8,128)(2,1)S(1)} %bitcast.43, bf16[128,1792]{1,0:T(8,128)(2,1)S(1)} %pad_maximum_fusion.1.refs_0_, bf16[128,1792]{1,0:T(8,128)(2,1)S(1)} %collective-permute-done.2.refs_1_, ...), custom_call_target="tpu_custom_call" | custom-call | tf_op jit(solution)/shard_map/pallas_call | solution.py:56
  100.1 1.9 %collective-permute-start.10 = (bf16[512,896]{1,0:T(8,128)(2,1)S(1)}, bf16[512,896]{1,0:T(8,128)(2,1)S(1)}, u32[]{:S(2)}, u32[]{:S(2)}) collective-permute-start(bf16[512,896]{1,0:T(8,128)(2,1)S(1)} %get-tuple-element.14), channel_id=1, source_target_pairs={{0,1},{1,0},{2,3},{3,2},{4,5},{5,4},{6,7},{7,6},{8,9},{9,8},{10,11... | collective-permute-start | bytes 2752520 | tf_op jit(solution)/shard_map/ppermute | solution.py:148
  102.0 2.4 %collective-permute-done.10.received = bf16[512,896]{1,0:T(8,128)(2,1)S(1)} collective-permute-done((bf16[512,896]{1,0:T(8,128)(2,1)S(1)}, bf16[512,896]{1,0:T(8,128)(2,1)S(1)}, u32[]{:S(2)}, u32[]{:S(2)}) %collective-permute-start.10) | collective-permute-done | bytes 917536 | tf_op jit(solution)/shard_map/ppermute | solution.py:148
  104.5 2.8 %shard_map.61 = bf16[512,896]{1,0:T(8,128)(2,1)} custom-call(s32[4,7]{1,0:T(4,128)S(1)} %copy-done.8, bf16[1024,512]{1,0:T(8,128)(2,1)S(1)} %get-tuple-element.13.in_rows, bf16[512,896]{1,0:T(8,128)(2,1)S(1)} %collective-permute-done.10.received, bf16[128,1792]{1,0:T(8,128)(2,1)S(1)} %pad_maximum_fusion.1.refs_0_, ...), custom_call_target="tpu_custom_call" | custom-call | tf_op jit(solution)/shard_map/pallas_call | solution.py:56
  107.3 10.8 %all-to-all-done = bf16[16,64,512]{2,1,0:T(8,128)(2,1)} async-done(((bf16[16,64,512]{2,1,0:T(8,128)(2,1)}), bf16[16,64,512]{2,1,0:T(8,128)(2,1)}, u32[]{:S(2)}, u32[]{:S(2)}) %all-to-all-start) | async-done | bytes 1048608 | tf_op jit(solution)/shard_map/all_to_all | solution.py:145
  118.2 2.0 %reduce_sum.12 = bf16[64,512]{1,0:T(8,128)(2,1)} reduce(bf16[16,64,512]{2,1,0:T(8,128)(2,1)} %all-to-all-done, bf16[]{:T(256)} %constant.231.clone.1), dimensions={0}, to_apply=%region_0.1 | reduce | flops 491520 | bytes 1114114 | tf_op jit(solution)/shard_map/reduce_sum | solution.py:152
  (54 shorter events, 7.5 us)
Async XLA Ops:
  0.6 12.1 %copy-start.11 = (bf16[512,896]{1,0:T(8,128)(2,1)S(1)}, bf16[512,896]{1,0:T(8,128)(2,1)}, u32[]{:S(2)}) copy-start(bf16[512,896]{1,0:T(8,128)(2,1)} %param.6) | copy-start | bytes 2752516
  4.1 18.7 %copy-start.9 = (bf16[64,896]{1,0:T(8,128)(2,1)}, bf16[64,896]{1,0:T(8,128)(2,1)S(1)}, u32[]{:S(2)}) copy-start(bf16[64,896]{1,0:T(8,128)(2,1)S(1)} %dynamic-slice_bitcast_fusion) | copy-start | bytes 344068
  4.1 8.6 %collective-permute-start = (bf16[64,1792]{1,0:T(8,128)(2,1)S(1)}, bf16[64,1792]{1,0:T(8,128)(2,1)S(1)}, u32[]{:S(2)}, u32[]{:S(2)}) collective-permute-start(bf16[64,1792]{1,0:T(8,128)(2,1)S(1)} %pad_maximum_fusion.2), channel_id=1, source_target_pairs={{0,64},{1,449},{64,0},{65,129},{128,192},{129,65},{192,128},{193,2... | collective-permute-start | bytes 688136 | tf_op jit(solution)/shard_map/ppermute | solution.py:42
  8.4 29.2 %collective-permute-start.5 = (bf16[64,1792]{1,0:T(8,128)(2,1)S(1)}, bf16[64,1792]{1,0:T(8,128)(2,1)S(1)}, u32[]{:S(2)}, u32[]{:S(2)}) collective-permute-start(bf16[64,1792]{1,0:T(8,128)(2,1)S(1)} %pad_maximum_fusion.2), channel_id=1, source_target_pairs={{0,32},{32,0},{1,33},{33,1},{2,34},{34,2},{3,35},{35,3},{4,36},{36... | collective-permute-start | bytes 688136 | tf_op jit(solution)/shard_map/ppermute | solution.py:126
  12.7 22.3 %copy-start.12 = (bf16[64,1792]{1,0:T(8,128)(2,1)}, bf16[64,1792]{1,0:T(8,128)(2,1)S(1)}, u32[]{:S(2)}) copy-start(bf16[64,1792]{1,0:T(8,128)(2,1)S(1)} %collective-permute-done) | copy-start | bytes 688132
  13.5 13.5 %copy-start.14 = (bf16[64,512]{1,0:T(8,128)(2,1)S(1)}, bf16[64,512]{1,0:T(8,128)(2,1)}, u32[]{:S(2)}) copy-start(bf16[64,512]{1,0:T(8,128)(2,1)} %param.4) | copy-start | bytes 196612
  14.6 39.9 %collective-permute-start.1 = (bf16[512,896]{0,1:T(8,128)(2,1)}, bf16[512,896]{0,1:T(8,128)(2,1)}, u32[]{:S(2)}, u32[]{:S(2)}) collective-permute-start(bf16[512,896]{0,1:T(8,128)(2,1)} %bitcast_multiply_fusion), channel_id=1, source_target_pairs={{0,1},{1,0},{2,3},{3,2},{4,5},{5,4},{6,7},{7,6},{8,9},{9,8},{10,11... | collective-permute-start | bytes 2752520 | tf_op jit(solution)/shard_map/ppermute | solution.py:133
  22.8 14.8 %collective-permute-start.2 = (bf16[128,1792]{1,0:T(8,128)(2,1)S(1)}, bf16[128,1792]{1,0:T(8,128)(2,1)S(1)}, u32[]{:S(2)}, u32[]{:S(2)}) collective-permute-start(bf16[128,1792]{1,0:T(8,128)(2,1)S(1)} %pad_maximum_fusion.1.refs_0_), channel_id=1, source_target_pairs={{0,448},{1,65},{64,128},{65,1},{128,64},{129,193},{192,256},{193,1... | collective-permute-start | bytes 1376264 | tf_op jit(solution)/shard_map/ppermute | solution.py:42
  27.8 18.9 %all-to-all-start.1 = ((bf16[4,64,512]{2,1,0:T(8,128)(2,1)}), bf16[4,64,512]{2,1,0:T(8,128)(2,1)S(1)}, u32[]{:S(2)}, u32[]{:S(2)}) async-start(bf16[4,64,512]{2,1,0:T(8,128)(2,1)} %broadcast_in_dim.7), calls=%async_computation.1 | async-start | bytes 524288 | tf_op jit(solution)/shard_map/all_to_all | solution.py:47
  35.0 11.7 %collective-permute-start.6 = (bf16[64,1792]{1,0:T(8,128)(2,1)S(1)}, bf16[64,1792]{1,0:T(8,128)(2,1)S(1)}, u32[]{:S(2)}, u32[]{:S(2)}) collective-permute-start(bf16[64,1792]{1,0:T(8,128)(2,1)S(1)} %collective-permute-done), channel_id=1, source_target_pairs={{0,32},{32,0},{1,33},{33,1},{2,34},{34,2},{3,35},{35,3},{4,36},{36... | collective-permute-start | bytes 688136 | tf_op jit(solution)/shard_map/ppermute | solution.py:131
  37.6 18.5 %collective-permute-start.7 = (bf16[128,1792]{1,0:T(8,128)(2,1)S(1)}, bf16[128,1792]{1,0:T(8,128)(2,1)S(1)}, u32[]{:S(2)}, u32[]{:S(2)}) collective-permute-start(bf16[128,1792]{1,0:T(8,128)(2,1)S(1)} %collective-permute-done.2.refs_1_), channel_id=1, source_target_pairs={{0,32},{32,0},{1,33},{33,1},{2,34},{34,2},{3,35},{35,3},{4,36},{36... | collective-permute-start | bytes 1376264 | tf_op jit(solution)/shard_map/ppermute | solution.py:135
  47.8 36.7 %all-to-all-start.2 = ((bf16[4,256,512]{2,1,0:T(8,128)(2,1)}), bf16[4,256,512]{2,1,0:T(8,128)(2,1)S(1)}, u32[]{:S(2)}, u32[]{:S(2)}) async-start(bf16[4,256,512]{2,1,0:T(8,128)(2,1)} %broadcast_in_dim.8), calls=%async_computation.2 | async-start | bytes 2097152 | tf_op jit(solution)/shard_map/all_to_all | solution.py:47
  52.6 10.4 %collective-permute-start.3 = (bf16[128,1792]{1,0:T(8,128)(2,1)S(1)}, bf16[128,1792]{1,0:T(8,128)(2,1)S(1)}, u32[]{:S(2)}, u32[]{:S(2)}) collective-permute-start(bf16[128,1792]{1,0:T(8,128)(2,1)S(1)} %collective-permute-done.2.refs_1_), channel_id=1, source_target_pairs={{0,64},{1,449},{64,0},{65,129},{128,192},{129,65},{192,128},{193,2... | collective-permute-start | bytes 1376264 | tf_op jit(solution)/shard_map/ppermute | solution.py:42
  56.1 14.1 %collective-permute-start.8 = (bf16[128,1792]{1,0:T(8,128)(2,1)S(1)}, bf16[128,1792]{1,0:T(8,128)(2,1)S(1)}, u32[]{:S(2)}, u32[]{:S(2)}) collective-permute-start(bf16[128,1792]{1,0:T(8,128)(2,1)S(1)} %collective-permute-done.7.refs_5_), channel_id=1, source_target_pairs={{0,64},{1,449},{64,0},{65,129},{128,192},{129,65},{192,128},{193,2... | collective-permute-start | bytes 1376264 | tf_op jit(solution)/shard_map/ppermute | solution.py:42
  60.9 5.8 %copy-start.10 = (bf16[64,896]{1,0:T(8,128)(2,1)S(1)}, bf16[64,896]{1,0:T(8,128)(2,1)}, u32[]{:S(2)}) copy-start(bf16[64,896]{1,0:T(8,128)(2,1)} %copy-done.9) | copy-start | bytes 344068
  60.9 5.8 %copy-start.13 = (bf16[64,1792]{1,0:T(8,128)(2,1)S(1)}, bf16[64,1792]{1,0:T(8,128)(2,1)}, u32[]{:S(2)}) copy-start(bf16[64,1792]{1,0:T(8,128)(2,1)} %copy-done.12) | copy-start | bytes 688132
  63.4 11.6 %collective-permute-start.4 = (bf16[128,1792]{1,0:T(8,128)(2,1)S(1)}, bf16[128,1792]{1,0:T(8,128)(2,1)S(1)}, u32[]{:S(2)}, u32[]{:S(2)}) collective-permute-start(bf16[128,1792]{1,0:T(8,128)(2,1)S(1)} %collective-permute-done.3.refs_2_), channel_id=1, source_target_pairs={{0,448},{1,65},{64,128},{65,1},{128,64},{129,193},{192,256},{193,1... | collective-permute-start | bytes 1376264 | tf_op jit(solution)/shard_map/ppermute | solution.py:42
  70.2 5.2 %copy-start = (bf16[128,1792]{1,0:T(8,128)(2,1)}, bf16[128,1792]{1,0:T(8,128)(2,1)S(1)}, u32[]{:S(2)}) copy-start(bf16[128,1792]{1,0:T(8,128)(2,1)S(1)} %collective-permute-done.8.refs_6_) | copy-start | bytes 1376260
  70.2 11.6 %collective-permute-start.9 = (bf16[128,1792]{1,0:T(8,128)(2,1)S(1)}, bf16[128,1792]{1,0:T(8,128)(2,1)S(1)}, u32[]{:S(2)}, u32[]{:S(2)}) collective-permute-start(bf16[128,1792]{1,0:T(8,128)(2,1)S(1)} %collective-permute-done.8.refs_6_), channel_id=1, source_target_pairs={{0,448},{1,65},{64,128},{65,1},{128,64},{129,193},{192,256},{193,1... | collective-permute-start | bytes 1376264 | tf_op jit(solution)/shard_map/ppermute | solution.py:42
  74.9 6.8 %copy-start.3 = (bf16[128,1792]{1,0:T(8,128)(2,1)}, bf16[128,1792]{1,0:T(8,128)(2,1)S(1)}, u32[]{:S(2)}) copy-start(bf16[128,1792]{1,0:T(8,128)(2,1)S(1)} %collective-permute-done.4.refs_3_) | copy-start | bytes 1376260
  82.2 0.8 copy-start.5
  84.6 33.6 %all-to-all-start = ((bf16[16,64,512]{2,1,0:T(8,128)(2,1)}), bf16[16,64,512]{2,1,0:T(8,128)(2,1)}, u32[]{:S(2)}, u32[]{:S(2)}) async-start(bf16[16,64,512]{2,1,0:T(8,128)(2,1)} %bitcast.18), calls=%async_computation | async-start | bytes 2097152 | tf_op jit(solution)/shard_map/all_to_all | solution.py:145
  95.2 1.0 copy-start.1
  96.2 1.0 copy-start.4
  97.2 1.0 copy-start.6
  98.2 6.3 %copy-start.2 = (bf16[128,1792]{1,0:T(8,128)(2,1)S(1)}, bf16[128,1792]{1,0:T(8,128)(2,1)}, u32[]{:S(2)}) copy-start(bf16[128,1792]{1,0:T(8,128)(2,1)} %copy-done) | copy-start | bytes 1376260
  98.2 6.3 %copy-start.7 = (bf16[128,1792]{1,0:T(8,128)(2,1)S(1)}, bf16[128,1792]{1,0:T(8,128)(2,1)}, u32[]{:S(2)}) copy-start(bf16[128,1792]{1,0:T(8,128)(2,1)} %copy-done.5) | copy-start | bytes 1376260
  98.2 6.3 %copy-start.8 = (s32[4,7]{1,0:T(4,128)S(1)}, s32[4,7]{1,0:T(4,128)}, u32[]{:S(2)}) copy-start(s32[4,7]{1,0:T(4,128)} %mask.1) | copy-start | bytes 340
  100.1 4.4 %collective-permute-start.10 = (bf16[512,896]{1,0:T(8,128)(2,1)S(1)}, bf16[512,896]{1,0:T(8,128)(2,1)S(1)}, u32[]{:S(2)}, u32[]{:S(2)}) collective-permute-start(bf16[512,896]{1,0:T(8,128)(2,1)S(1)} %get-tuple-element.14), channel_id=1, source_target_pairs={{0,1},{1,0},{2,3},{3,2},{4,5},{5,4},{6,7},{7,6},{8,9},{9,8},{10,11... | collective-permute-start | bytes 2752520 | tf_op jit(solution)/shard_map/ppermute | solution.py:148

commit v5 on v4

--- a/solution.py
+++ b/solution.py
@@ -134,12 +134,12 @@
     wide = lax.optimization_barrier(wide)
     b2 = lax.ppermute(a2, "y_lo", SWAP)
     a3 = swap(a2, "z", near)
-    quad = all_copies(after(line, a2, b1), "x").reshape(16, rows, width)
+    quad = all_copies(after(line, a2), "x").reshape(16, rows, width)
     b3 = swap(after(b2, wide), "z", near)
     a4 = swap(a3, "z", next_pair)
     b4 = swap(b3, "z", next_pair)
 
-    parts = (pair, a2, a3, a4, jnp.concatenate([b0, b1], axis=0), b2, b3, b4)
+    parts = (pair, a2, a3, a4, jnp.concatenate([after(b0, b3), after(b1, b3)], axis=0), b2, b3, b4)
     value = [matmul(part, wide, (1, 1)).astype(jnp.bfloat16) for part in parts]
     (value,) = call(place_kernel, [(16 * rows, width)], (order, *value), 1)
     value = lax.all_to_all(value.reshape(16, rows, width), ("x", "y_hi"), 0, 0, tiled=True)

time: 121 us -> 121 us (level)
  starting transfers between devices: 61 us -> 57.8 us
  local copies, waits for them, and re-layouts: 7.66 us -> 9.71 us
  waiting for transfers between devices: 33.1 us -> 31.5 us
    ppermute x1, waiting for transfers between devices: 5.82 us -> 0.01 us  [shards(): b1 = lax.ppermute(a1, 'y_lo', SWAP)]
    ppermute x6, waiting for transfers between devices: 14 us -> 18.2 us  [swap(): return lax.ppermute(value, (axis, 'core'), pairs)]
    all_to_all x1, starting transfers between devices: 10.6 us -> 7.17 us  [shards(): lax.all_to_all(value.reshape(16, rows, width), ('x', 'y_hi'), 0, 0, tiled...]
    all_to_all x2, waiting for transfers between devices: 0.01 us -> 2.18 us  [all_copies(): lax.all_to_all(copies, axis, 0, 0, tiled=True)]
    all_to_all x1, waiting for transfers between devices: 10.8 us -> 8.75 us  [shards(): lax.all_to_all(value.reshape(16, rows, width), ('x', 'y_hi'), 0, 0, tiled...]
    ppermute x6, starting transfers between devices: 19.1 us -> 20.5 us  [swap(): return lax.ppermute(value, (axis, 'core'), pairs)]
    unnamed x31 -> x23, local copies, waits for them, and re-layouts: 3.88 us -> 4.97 us
  transfers between devices with their start and end apart: 14 -> 14, of which waited for: 7 -> 7; matrix products, arithmetic and copies ran while one was open for 8% -> 10% of each run, Pallas kernels for 5% -> 5%
where the time goes in v5:
time: 121 us; the launch traced here: 120 us
  starting transfers between devices  57.8 us (48%)
  waiting for transfers between devices  31.5 us (26%)
  local copies, waits for them, and re-layouts  9.71 us (8%)
  other arithmetic  6.34 us (5%)
  Pallas kernels  6.28 us (5%)
  matrix products  4.19 us (3%)
  blocking collectives  2.48 us (2%)
  between operations  1.51 us (1%)
    ppermute x6, starting transfers between devices, swap(): return lax.ppermute(value, (axis, 'core'), pairs)  20.5 us
    ppermute x6, waiting for transfers between devices, swap(): return lax.ppermute(value, (axis, 'core'), pairs)  18.2 us
    all_to_all x2, starting transfers between devices, all_copies(): lax.all_to_all(copies, axis, 0, 0, tiled=True)  11.9 us
    all_to_all x1, waiting for transfers between devices, shards(): lax.all_to_all(value.reshape(16, rows, width), ('x', 'y_hi'), 0, 0, tiled...  8.75 us
    ppermute x1, starting transfers between devices, shards(): wide = jnp.concatenate([masked, lax.ppermute(masked, 'core', SWAP)], axis=1)  7.83 us
    all_to_all x1, starting transfers between devices, shards(): lax.all_to_all(value.reshape(16, rows, width), ('x', 'y_hi'), 0, 0, tiled...  7.17 us
    pallas_call x3, Pallas kernels, call(): pl.pallas_call(kernel, out_shape=[jax.ShapeDtypeStruct(shape, jnp.bfloat1...  6.28 us
    unnamed x23, local copies, waits for them, and re-layouts  4.97 us
  transfers between devices with their start and end apart: 14, of which 7 were waited for; matrix products, arithmetic and copies ran while one was open for 10% of the time, Pallas kernels for 5%

profile of v5, /device:TPU:6, one launch (start us, length us, event | category | flops | bytes accessed | tf_op | source)
XLA Modules:
  0.0 119.8 jit_solution(10923190643666819077)
XLA Ops:
  0.6 2.5 %all-gather = bf16[256,896]{1,0:T(8,128)(2,1)S(1)} all-gather(bf16[128,896]{1,0:T(8,128)(2,1)} %param.5), channel_id=2, replica_groups=mesh['z'=8,'y_lo'=2,'x'=4,'y_hi'=4,'core'=2] {'core'}, dimensions={0}, use_global_device_ids=true | all-gather | bytes 688128 | tf_op jit(solution)/shard_map/all_gather | solution.py:121
  4.1 4.3 %collective-permute-start = (bf16[64,1792]{1,0:T(8,128)(2,1)S(1)}, bf16[64,1792]{1,0:T(8,128)(2,1)}, u32[]{:S(2)}, u32[]{:S(2)}) collective-permute-start(bf16[64,1792]{1,0:T(8,128)(2,1)S(1)} %pad_maximum_fusion.2), channel_id=1, source_target_pairs={{0,64},{1,449},{64,0},{65,129},{128,192},{129,65},{192,128},{193,2... | collective-permute-start | bytes 688136 | tf_op jit(solution)/shard_map/ppermute | solution.py:42
  9.2 3.3 %collective-permute-done = bf16[64,1792]{1,0:T(8,128)(2,1)} collective-permute-done((bf16[64,1792]{1,0:T(8,128)(2,1)S(1)}, bf16[64,1792]{1,0:T(8,128)(2,1)}, u32[]{:S(2)}, u32[]{:S(2)}) %collective-permute-start) | collective-permute-done | bytes 229408 | tf_op jit(solution)/shard_map/ppermute | solution.py:42
  13.3 1.1 bitcast_multiply_fusion
  14.4 7.8 %collective-permute-start.1 = (bf16[512,896]{0,1:T(8,128)(2,1)}, bf16[512,896]{0,1:T(8,128)(2,1)}, u32[]{:S(2)}, u32[]{:S(2)}) collective-permute-start(bf16[512,896]{0,1:T(8,128)(2,1)} %bitcast_multiply_fusion), channel_id=1, source_target_pairs={{0,1},{1,0},{2,3},{3,2},{4,5},{5,4},{6,7},{7,6},{8,9},{9,8},{10,11... | collective-permute-start | bytes 2752520 | tf_op jit(solution)/shard_map/ppermute | solution.py:133
  23.2 4.9 %collective-permute-start.2 = (bf16[128,1792]{1,0:T(8,128)(2,1)S(1)}, bf16[128,1792]{1,0:T(8,128)(2,1)S(1)}, u32[]{:S(2)}, u32[]{:S(2)}) collective-permute-start(bf16[128,1792]{1,0:T(8,128)(2,1)S(1)} %pad_maximum_fusion.1.refs_0_), channel_id=1, source_target_pairs={{0,448},{1,65},{64,128},{65,1},{128,64},{129,193},{192,256},{193,1... | collective-permute-start | bytes 1376264 | tf_op jit(solution)/shard_map/ppermute | solution.py:42
  28.8 7.1 %all-to-all-start.1 = ((bf16[4,64,512]{2,1,0:T(8,128)(2,1)}), bf16[4,64,512]{2,1,0:T(8,128)(2,1)S(1)}, u32[]{:S(2)}, u32[]{:S(2)}) async-start(bf16[4,64,512]{2,1,0:T(8,128)(2,1)} %broadcast_in_dim.7), calls=%async_computation.1 | async-start | bytes 524288 | tf_op jit(solution)/shard_map/all_to_all | solution.py:47
  35.9 2.6 %collective-permute-start.6 = (bf16[128,1792]{1,0:T(8,128)(2,1)S(1)}, bf16[128,1792]{1,0:T(8,128)(2,1)S(1)}, u32[]{:S(2)}, u32[]{:S(2)}) collective-permute-start(bf16[128,1792]{1,0:T(8,128)(2,1)S(1)} %collective-permute-done.2.refs_1_), channel_id=1, source_target_pairs={{0,32},{32,0},{1,33},{33,1},{2,34},{34,2},{3,35},{35,3},{4,36},{36... | collective-permute-start | bytes 1376264 | tf_op jit(solution)/shard_map/ppermute | solution.py:135
  38.5 3.3 %collective-permute-start.5 = (bf16[64,1792]{1,0:T(8,128)(2,1)S(1)}, bf16[64,1792]{1,0:T(8,128)(2,1)}, u32[]{:S(2)}, u32[]{:S(2)}) collective-permute-start(bf16[64,1792]{1,0:T(8,128)(2,1)S(1)} %pad_maximum_fusion.2), channel_id=1, source_target_pairs={{0,32},{32,0},{1,33},{33,1},{2,34},{34,2},{3,35},{35,3},{4,36},{36... | collective-permute-start | bytes 688136 | tf_op jit(solution)/shard_map/ppermute | solution.py:126
  42.4 2.6 %collective-permute-start.8 = (bf16[64,1792]{1,0:T(8,128)(2,1)}, bf16[64,1792]{1,0:T(8,128)(2,1)}, u32[]{:S(2)}, u32[]{:S(2)}) collective-permute-start(bf16[64,1792]{1,0:T(8,128)(2,1)} %collective-permute-done), channel_id=1, source_target_pairs={{0,32},{32,0},{1,33},{33,1},{2,34},{34,2},{3,35},{35,3},{4,36},{36... | collective-permute-start | bytes 688136 | tf_op jit(solution)/shard_map/ppermute | solution.py:131
  45.0 2.2 %all-to-all-done.1 = bf16[4,64,512]{2,1,0:T(8,128)(2,1)S(1)} async-done(((bf16[4,64,512]{2,1,0:T(8,128)(2,1)}), bf16[4,64,512]{2,1,0:T(8,128)(2,1)S(1)}, u32[]{:S(2)}, u32[]{:S(2)}) %all-to-all-start.1) | async-done | bytes 262176 | tf_op jit(solution)/shard_map/all_to_all | solution.py:47
  47.2 1.1 broadcast_in_dim.8
  48.3 4.8 %all-to-all-start.2 = ((bf16[4,256,512]{2,1,0:T(8,128)(2,1)}), bf16[4,256,512]{2,1,0:T(8,128)(2,1)S(1)}, u32[]{:S(2)}, u32[]{:S(2)}) async-start(bf16[4,256,512]{2,1,0:T(8,128)(2,1)} %broadcast_in_dim.8), calls=%async_computation.2 | async-start | bytes 2097152 | tf_op jit(solution)/shard_map/all_to_all | solution.py:47
  53.0 1.9 %collective-permute-start.3 = (bf16[128,1792]{1,0:T(8,128)(2,1)S(1)}, bf16[128,1792]{1,0:T(8,128)(2,1)S(1)}, u32[]{:S(2)}, u32[]{:S(2)}) collective-permute-start(bf16[128,1792]{1,0:T(8,128)(2,1)S(1)} %collective-permute-done.2.refs_1_), channel_id=1, source_target_pairs={{0,64},{1,449},{64,0},{65,129},{128,192},{129,65},{192,128},{193,2... | collective-permute-start | bytes 1376264 | tf_op jit(solution)/shard_map/ppermute | solution.py:42
  55.0 1.6 %pad_maximum_fusion = bf16[512,1792]{0,1:T(8,128)(2,1)S(1)} fusion(bf16[512,896]{0,1:T(8,128)(2,1)} %collective-permute-done.1, bf16[512,896]{0,1:T(8,128)(2,1)} %bitcast_multiply_fusion), kind=kLoop, calls=%fused_computation | loop fusion | flops 3670016 | bytes 3670016 | tf_op jit(solution)/shard_map/concatenate | solution.py:133
  56.6 3.9 %collective-permute-start.7 = (bf16[128,1792]{1,0:T(8,128)(2,1)S(1)}, bf16[128,1792]{1,0:T(8,128)(2,1)S(1)}, u32[]{:S(2)}, u32[]{:S(2)}) collective-permute-start(bf16[128,1792]{1,0:T(8,128)(2,1)S(1)} %collective-permute-done.6.refs_5_), channel_id=1, source_target_pairs={{0,64},{1,449},{64,0},{65,129},{128,192},{129,65},{192,128},{193,2... | collective-permute-start | bytes 1376264 | tf_op jit(solution)/shard_map/ppermute | solution.py:42
  60.9 2.5 %collective-permute-done.3.refs_2_ = bf16[128,1792]{1,0:T(8,128)(2,1)S(1)} collective-permute-done((bf16[128,1792]{1,0:T(8,128)(2,1)S(1)}, bf16[128,1792]{1,0:T(8,128)(2,1)S(1)}, u32[]{:S(2)}, u32[]{:S(2)}) %collective-permute-start.3) | collective-permute-done | bytes 458784 | tf_op jit(solution)/shard_map/ppermute | solution.py:42
  63.8 3.4 %collective-permute-start.4 = (bf16[128,1792]{1,0:T(8,128)(2,1)S(1)}, bf16[128,1792]{1,0:T(8,128)(2,1)S(1)}, u32[]{:S(2)}, u32[]{:S(2)}) collective-permute-start(bf16[128,1792]{1,0:T(8,128)(2,1)S(1)} %collective-permute-done.3.refs_2_), channel_id=1, source_target_pairs={{0,448},{1,65},{64,128},{65,1},{128,64},{129,193},{192,256},{193,1... | collective-permute-start | bytes 1376264 | tf_op jit(solution)/shard_map/ppermute | solution.py:42
  67.7 1.3 %convolution_convert_fusion.7.refs_0_ = bf16[128,512]{1,0:T(8,128)(2,1)S(1)} fusion(bf16[512,1792]{0,1:T(8,128)(2,1)S(1)} %pad_maximum_fusion, bf16[64,1792]{1,0:T(8,128)(2,1)} %collective-permute-done, bf16[64,896]{1,0:T(8,128)(2,1)S(1)} %dynamic-slice_bitcast_fusion, bf16[64,896]{1,0:T(8,128)(2,1)S(1)} %constant_dynamic-slice_fusion), kind=kOutput, calls=%fused_computation.8 | convolution fusion | flops 236322816 | bytes 2424832 | tf_op jit(solution)/shard_map/dot_general | solution.py:24
  69.0 4.2 %collective-permute-done.7.refs_6_ = bf16[128,1792]{1,0:T(8,128)(2,1)S(1)} collective-permute-done((bf16[128,1792]{1,0:T(8,128)(2,1)S(1)}, bf16[128,1792]{1,0:T(8,128)(2,1)S(1)}, u32[]{:S(2)}, u32[]{:S(2)}) %collective-permute-start.7) | collective-permute-done | bytes 458784 | tf_op jit(solution)/shard_map/ppermute | solution.py:42
  73.3 1.1 constant_dynamic-update-slice_fusion.1
  75.3 2.2 %collective-permute-start.9 = (bf16[128,1792]{1,0:T(8,128)(2,1)S(1)}, bf16[128,1792]{1,0:T(8,128)(2,1)S(1)}, u32[]{:S(2)}, u32[]{:S(2)}) collective-permute-start(bf16[128,1792]{1,0:T(8,128)(2,1)S(1)} %collective-permute-done.7.refs_6_), channel_id=1, source_target_pairs={{0,448},{1,65},{64,128},{65,1},{128,64},{129,193},{192,256},{193,1... | collective-permute-start | bytes 1376264 | tf_op jit(solution)/shard_map/ppermute | solution.py:42
  78.8 8.1 %collective-permute-done.9.refs_7_ = bf16[128,1792]{1,0:T(8,128)(2,1)S(1)} collective-permute-done((bf16[128,1792]{1,0:T(8,128)(2,1)S(1)}, bf16[128,1792]{1,0:T(8,128)(2,1)S(1)}, u32[]{:S(2)}, u32[]{:S(2)}) %collective-permute-start.9) | collective-permute-done | bytes 458784 | tf_op jit(solution)/shard_map/ppermute | solution.py:42
  88.1 1.6 %shard_map.59 = bf16[1024,512]{1,0:T(8,128)(2,1)} custom-call(s32[16]{0:T(128)S(1)} %stack.67.order, bf16[128,512]{1,0:T(8,128)(2,1)S(1)} %convolution_convert_fusion.7.refs_0_, bf16[128,512]{1,0:T(8,128)(2,1)S(1)} %convolution_convert_fusion.6.refs_1_, bf16[128,512]{1,0:T(8,128)(2,1)S(1)} %convolution_convert_fusion.5.refs_2_, ...), custom_call_target="tpu_custom_call" | custom-call | tf_op jit(solution)/shard_map/pallas_call | solution.py:56
  89.7 7.2 %all-to-all-start = ((bf16[16,64,512]{2,1,0:T(8,128)(2,1)}), bf16[16,64,512]{2,1,0:T(8,128)(2,1)}, u32[]{:S(2)}, u32[]{:S(2)}) async-start(bf16[16,64,512]{2,1,0:T(8,128)(2,1)} %bitcast.18), calls=%async_computation | async-start | bytes 2097152 | tf_op jit(solution)/shard_map/all_to_all | solution.py:145
  97.9 1.0 copy-done.4
  99.9 1.9 %shard_map.60 = (bf16[1024,512]{1,0:T(8,128)(2,1)S(1)}, bf16[512,896]{1,0:T(8,128)(2,1)S(1)}) custom-call(s32[16]{0:T(128)S(1)} %stack.67.order, bf16[16,64,512]{2,1,0:T(8,128)(2,1)S(1)} %bitcast.43, bf16[128,1792]{1,0:T(8,128)(2,1)S(1)} %pad_maximum_fusion.1.refs_0_, bf16[128,1792]{1,0:T(8,128)(2,1)S(1)} %collective-permute-done.2.refs_1_, ...), custom_call_target="tpu_custom_call" | custom-call | tf_op jit(solution)/shard_map/pallas_call | solution.py:56
  101.8 1.9 %collective-permute-start.10 = (bf16[512,896]{1,0:T(8,128)(2,1)S(1)}, bf16[512,896]{1,0:T(8,128)(2,1)S(1)}, u32[]{:S(2)}, u32[]{:S(2)}) collective-permute-start(bf16[512,896]{1,0:T(8,128)(2,1)S(1)} %get-tuple-element.18), channel_id=1, source_target_pairs={{0,1},{1,0},{2,3},{3,2},{4,5},{5,4},{6,7},{7,6},{8,9},{9,8},{10,11... | collective-permute-start | bytes 2752520 | tf_op jit(solution)/shard_map/ppermute | solution.py:148
  103.7 2.4 %collective-permute-done.10.received = bf16[512,896]{1,0:T(8,128)(2,1)S(1)} collective-permute-done((bf16[512,896]{1,0:T(8,128)(2,1)S(1)}, bf16[512,896]{1,0:T(8,128)(2,1)S(1)}, u32[]{:S(2)}, u32[]{:S(2)}) %collective-permute-start.10) | collective-permute-done | bytes 917536 | tf_op jit(solution)/shard_map/ppermute | solution.py:148
  106.2 2.8 %shard_map.61 = bf16[512,896]{1,0:T(8,128)(2,1)} custom-call(s32[4,7]{1,0:T(4,128)S(1)} %copy-done.8, bf16[1024,512]{1,0:T(8,128)(2,1)S(1)} %get-tuple-element.17.in_rows, bf16[512,896]{1,0:T(8,128)(2,1)S(1)} %collective-permute-done.10.received, bf16[128,1792]{1,0:T(8,128)(2,1)S(1)} %pad_maximum_fusion.1.refs_0_, ...), custom_call_target="tpu_custom_call" | custom-call | tf_op jit(solution)/shard_map/pallas_call | solution.py:56
  109.0 8.8 %all-to-all-done = bf16[16,64,512]{2,1,0:T(8,128)(2,1)} async-done(((bf16[16,64,512]{2,1,0:T(8,128)(2,1)}), bf16[16,64,512]{2,1,0:T(8,128)(2,1)}, u32[]{:S(2)}, u32[]{:S(2)}) %all-to-all-start) | async-done | bytes 1048608 | tf_op jit(solution)/shard_map/all_to_all | solution.py:145
  117.8 2.0 %reduce_sum.12 = bf16[64,512]{1,0:T(8,128)(2,1)} reduce(bf16[16,64,512]{2,1,0:T(8,128)(2,1)} %all-to-all-done, bf16[]{:T(256)} %constant.231.clone.1), dimensions={0}, to_apply=%region_0.1 | reduce | flops 491520 | bytes 1114114 | tf_op jit(solution)/shard_map/reduce_sum | solution.py:152
  (46 shorter events, 11.0 us)
Async XLA Ops:
  0.6 11.8 %copy-start.9 = (bf16[512,896]{1,0:T(8,128)(2,1)S(1)}, bf16[512,896]{1,0:T(8,128)(2,1)}, u32[]{:S(2)}) copy-start(bf16[512,896]{1,0:T(8,128)(2,1)} %param.6) | copy-start | bytes 2752516
  4.1 8.4 %collective-permute-start = (bf16[64,1792]{1,0:T(8,128)(2,1)S(1)}, bf16[64,1792]{1,0:T(8,128)(2,1)}, u32[]{:S(2)}, u32[]{:S(2)}) collective-permute-start(bf16[64,1792]{1,0:T(8,128)(2,1)S(1)} %pad_maximum_fusion.2), channel_id=1, source_target_pairs={{0,64},{1,449},{64,0},{65,129},{128,192},{129,65},{192,128},{193,2... | collective-permute-start | bytes 688136 | tf_op jit(solution)/shard_map/ppermute | solution.py:42
  13.3 14.8 %copy-start.10 = (bf16[64,512]{1,0:T(8,128)(2,1)S(1)}, bf16[64,512]{1,0:T(8,128)(2,1)}, u32[]{:S(2)}) copy-start(bf16[64,512]{1,0:T(8,128)(2,1)} %param.4) | copy-start | bytes 196612
  14.4 40.6 %collective-permute-start.1 = (bf16[512,896]{0,1:T(8,128)(2,1)}, bf16[512,896]{0,1:T(8,128)(2,1)}, u32[]{:S(2)}, u32[]{:S(2)}) collective-permute-start(bf16[512,896]{0,1:T(8,128)(2,1)} %bitcast_multiply_fusion), channel_id=1, source_target_pairs={{0,1},{1,0},{2,3},{3,2},{4,5},{5,4},{6,7},{7,6},{8,9},{9,8},{10,11... | collective-permute-start | bytes 2752520 | tf_op jit(solution)/shard_map/ppermute | solution.py:133
  23.2 12.7 %collective-permute-start.2 = (bf16[128,1792]{1,0:T(8,128)(2,1)S(1)}, bf16[128,1792]{1,0:T(8,128)(2,1)S(1)}, u32[]{:S(2)}, u32[]{:S(2)}) collective-permute-start(bf16[128,1792]{1,0:T(8,128)(2,1)S(1)} %pad_maximum_fusion.1.refs_0_), channel_id=1, source_target_pairs={{0,448},{1,65},{64,128},{65,1},{128,64},{129,193},{192,256},{193,1... | collective-permute-start | bytes 1376264 | tf_op jit(solution)/shard_map/ppermute | solution.py:42
  28.8 18.4 %all-to-all-start.1 = ((bf16[4,64,512]{2,1,0:T(8,128)(2,1)}), bf16[4,64,512]{2,1,0:T(8,128)(2,1)S(1)}, u32[]{:S(2)}, u32[]{:S(2)}) async-start(bf16[4,64,512]{2,1,0:T(8,128)(2,1)} %broadcast_in_dim.7), calls=%async_computation.1 | async-start | bytes 524288 | tf_op jit(solution)/shard_map/all_to_all | solution.py:47
  35.9 20.6 %collective-permute-start.6 = (bf16[128,1792]{1,0:T(8,128)(2,1)S(1)}, bf16[128,1792]{1,0:T(8,128)(2,1)S(1)}, u32[]{:S(2)}, u32[]{:S(2)}) collective-permute-start(bf16[128,1792]{1,0:T(8,128)(2,1)S(1)} %collective-permute-done.2.refs_1_), channel_id=1, source_target_pairs={{0,32},{32,0},{1,33},{33,1},{2,34},{34,2},{3,35},{35,3},{4,36},{36... | collective-permute-start | bytes 1376264 | tf_op jit(solution)/shard_map/ppermute | solution.py:135
  38.5 30.5 %collective-permute-start.5 = (bf16[64,1792]{1,0:T(8,128)(2,1)S(1)}, bf16[64,1792]{1,0:T(8,128)(2,1)}, u32[]{:S(2)}, u32[]{:S(2)}) collective-permute-start(bf16[64,1792]{1,0:T(8,128)(2,1)S(1)} %pad_maximum_fusion.2), channel_id=1, source_target_pairs={{0,32},{32,0},{1,33},{33,1},{2,34},{34,2},{3,35},{35,3},{4,36},{36... | collective-permute-start | bytes 688136 | tf_op jit(solution)/shard_map/ppermute | solution.py:126
  42.4 32.0 %collective-permute-start.8 = (bf16[64,1792]{1,0:T(8,128)(2,1)}, bf16[64,1792]{1,0:T(8,128)(2,1)}, u32[]{:S(2)}, u32[]{:S(2)}) collective-permute-start(bf16[64,1792]{1,0:T(8,128)(2,1)} %collective-permute-done), channel_id=1, source_target_pairs={{0,32},{32,0},{1,33},{33,1},{2,34},{34,2},{3,35},{35,3},{4,36},{36... | collective-permute-start | bytes 688136 | tf_op jit(solution)/shard_map/ppermute | solution.py:131
  48.3 41.4 %all-to-all-start.2 = ((bf16[4,256,512]{2,1,0:T(8,128)(2,1)}), bf16[4,256,512]{2,1,0:T(8,128)(2,1)S(1)}, u32[]{:S(2)}, u32[]{:S(2)}) async-start(bf16[4,256,512]{2,1,0:T(8,128)(2,1)} %broadcast_in_dim.8), calls=%async_computation.2 | async-start | bytes 2097152 | tf_op jit(solution)/shard_map/all_to_all | solution.py:47
  53.0 10.4 %collective-permute-start.3 = (bf16[128,1792]{1,0:T(8,128)(2,1)S(1)}, bf16[128,1792]{1,0:T(8,128)(2,1)S(1)}, u32[]{:S(2)}, u32[]{:S(2)}) collective-permute-start(bf16[128,1792]{1,0:T(8,128)(2,1)S(1)} %collective-permute-done.2.refs_1_), channel_id=1, source_target_pairs={{0,64},{1,449},{64,0},{65,129},{128,192},{129,65},{192,128},{193,2... | collective-permute-start | bytes 1376264 | tf_op jit(solution)/shard_map/ppermute | solution.py:42
  56.6 16.7 %collective-permute-start.7 = (bf16[128,1792]{1,0:T(8,128)(2,1)S(1)}, bf16[128,1792]{1,0:T(8,128)(2,1)S(1)}, u32[]{:S(2)}, u32[]{:S(2)}) collective-permute-start(bf16[128,1792]{1,0:T(8,128)(2,1)S(1)} %collective-permute-done.6.refs_5_), channel_id=1, source_target_pairs={{0,64},{1,449},{64,0},{65,129},{128,192},{129,65},{192,128},{193,2... | collective-permute-start | bytes 1376264 | tf_op jit(solution)/shard_map/ppermute | solution.py:42
  63.8 14.5 %collective-permute-start.4 = (bf16[128,1792]{1,0:T(8,128)(2,1)S(1)}, bf16[128,1792]{1,0:T(8,128)(2,1)S(1)}, u32[]{:S(2)}, u32[]{:S(2)}) collective-permute-start(bf16[128,1792]{1,0:T(8,128)(2,1)S(1)} %collective-permute-done.3.refs_2_), channel_id=1, source_target_pairs={{0,448},{1,65},{64,128},{65,1},{128,64},{129,193},{192,256},{193,1... | collective-permute-start | bytes 1376264 | tf_op jit(solution)/shard_map/ppermute | solution.py:42
  73.3 5.1 %copy-start = (bf16[128,1792]{1,0:T(8,128)(2,1)}, bf16[128,1792]{1,0:T(8,128)(2,1)S(1)}, u32[]{:S(2)}) copy-start(bf16[128,1792]{1,0:T(8,128)(2,1)S(1)} %collective-permute-done.7.refs_6_) | copy-start | bytes 1376260
  75.3 11.6 %collective-permute-start.9 = (bf16[128,1792]{1,0:T(8,128)(2,1)S(1)}, bf16[128,1792]{1,0:T(8,128)(2,1)S(1)}, u32[]{:S(2)}, u32[]{:S(2)}) collective-permute-start(bf16[128,1792]{1,0:T(8,128)(2,1)S(1)} %collective-permute-done.7.refs_6_), channel_id=1, source_target_pairs={{0,448},{1,65},{64,128},{65,1},{128,64},{129,193},{192,256},{193,1... | collective-permute-start | bytes 1376264 | tf_op jit(solution)/shard_map/ppermute | solution.py:42
  78.4 8.5 %copy-start.3 = (bf16[128,1792]{1,0:T(8,128)(2,1)}, bf16[128,1792]{1,0:T(8,128)(2,1)S(1)}, u32[]{:S(2)}) copy-start(bf16[128,1792]{1,0:T(8,128)(2,1)S(1)} %collective-permute-done.4.refs_3_) | copy-start | bytes 1376260
  87.3 0.8 copy-start.5
  89.7 28.1 %all-to-all-start = ((bf16[16,64,512]{2,1,0:T(8,128)(2,1)}), bf16[16,64,512]{2,1,0:T(8,128)(2,1)}, u32[]{:S(2)}, u32[]{:S(2)}) async-start(bf16[16,64,512]{2,1,0:T(8,128)(2,1)} %bitcast.18), calls=%async_computation | async-start | bytes 2097152 | tf_op jit(solution)/shard_map/all_to_all | solution.py:145
  96.9 1.0 copy-start.1
  97.9 1.0 copy-start.4
  98.9 1.0 copy-start.6
  99.9 6.2 %copy-start.2 = (bf16[128,1792]{1,0:T(8,128)(2,1)S(1)}, bf16[128,1792]{1,0:T(8,128)(2,1)}, u32[]{:S(2)}) copy-start(bf16[128,1792]{1,0:T(8,128)(2,1)} %copy-done) | copy-start | bytes 1376260
  99.9 6.2 %copy-start.7 = (bf16[128,1792]{1,0:T(8,128)(2,1)S(1)}, bf16[128,1792]{1,0:T(8,128)(2,1)}, u32[]{:S(2)}) copy-start(bf16[128,1792]{1,0:T(8,128)(2,1)} %copy-done.5) | copy-start | bytes 1376260
  99.9 6.2 %copy-start.8 = (s32[4,7]{1,0:T(4,128)S(1)}, s32[4,7]{1,0:T(4,128)}, u32[]{:S(2)}) copy-start(s32[4,7]{1,0:T(4,128)} %mask.1) | copy-start | bytes 340
  101.8 4.4 %collective-permute-start.10 = (bf16[512,896]{1,0:T(8,128)(2,1)S(1)}, bf16[512,896]{1,0:T(8,128)(2,1)S(1)}, u32[]{:S(2)}, u32[]{:S(2)}) collective-permute-start(bf16[512,896]{1,0:T(8,128)(2,1)S(1)} %get-tuple-element.18), channel_id=1, source_target_pairs={{0,1},{1,0},{2,3},{3,2},{4,5},{5,4},{6,7},{7,6},{8,9},{9,8},{10,11... | collective-permute-start | bytes 2752520 | tf_op jit(solution)/shard_map/ppermute | solution.py:148

commit v6 on v5

--- a/solution.py
+++ b/solution.py
@@ -139,7 +139,7 @@
     a4 = swap(a3, "z", next_pair)
     b4 = swap(b3, "z", next_pair)
 
-    parts = (pair, a2, a3, a4, jnp.concatenate([after(b0, b3), after(b1, b3)], axis=0), b2, b3, b4)
+    parts = (pair, a2, a3, a4, jnp.concatenate([b0, after(b1, b3)], axis=0), b2, b3, b4)
     value = [matmul(part, wide, (1, 1)).astype(jnp.bfloat16) for part in parts]
     (value,) = call(place_kernel, [(16 * rows, width)], (order, *value), 1)
     value = lax.all_to_all(value.reshape(16, rows, width), ("x", "y_hi"), 0, 0, tiled=True)

time: 121 us -> 122 us (level)
  the two profiles are of different devices: /device:TPU:6 before, /device:TPU:2 now
where the time goes in v6:
time: 122 us; the launch traced here: 121 us
  starting transfers between devices  54.6 us (45%)
  waiting for transfers between devices  36.9 us (30%)
  local copies, waits for them, and re-layouts  8.77 us (7%)
  other arithmetic  6.34 us (5%)
  Pallas kernels  6.27 us (5%)
  matrix products  4.18 us (3%)
  blocking collectives  2.48 us (2%)
    ppermute x6, starting transfers between devices, swap(): return lax.ppermute(value, (axis, 'core'), pairs)  19 us
    ppermute x6, waiting for transfers between devices, swap(): return lax.ppermute(value, (axis, 'core'), pairs)  18.9 us
    all_to_all x2, starting transfers between devices, all_copies(): lax.all_to_all(copies, axis, 0, 0, tiled=True)  11 us
    all_to_all x1, waiting for transfers between devices, shards(): lax.all_to_all(value.reshape(16, rows, width), ('x', 'y_hi'), 0, 0, tiled...  9.65 us
    ppermute x1, starting transfers between devices, shards(): wide = jnp.concatenate([masked, lax.ppermute(masked, 'core', SWAP)], axis=1)  7.83 us
    pallas_call x3, Pallas kernels, call(): pl.pallas_call(kernel, out_shape=[jax.ShapeDtypeStruct(shape, jnp.bfloat1...  6.27 us
    all_to_all x2, waiting for transfers between devices, all_copies(): lax.all_to_all(copies, axis, 0, 0, tiled=True)  5.93 us
    all_to_all x1, starting transfers between devices, shards(): lax.all_to_all(value.reshape(16, rows, width), ('x', 'y_hi'), 0, 0, tiled...  5.49 us
  transfers between devices with their start and end apart: 14, of which 7 were waited for; matrix products, arithmetic and copies ran while one was open for 9% of the time, Pallas kernels for 5%

profile of v6, /device:TPU:2, one launch (start us, length us, event | category | flops | bytes accessed | tf_op | source)
XLA Modules:
  0.0 120.6 jit_solution(16783094163923254720)
XLA Ops:
  0.6 2.5 %all-gather = bf16[256,896]{1,0:T(8,128)(2,1)S(1)} all-gather(bf16[128,896]{1,0:T(8,128)(2,1)} %param.5), channel_id=2, replica_groups=mesh['z'=8,'y_lo'=2,'x'=4,'y_hi'=4,'core'=2] {'core'}, dimensions={0}, use_global_device_ids=true | all-gather | bytes 688128 | tf_op jit(solution)/shard_map/all_gather | solution.py:121
  4.1 4.3 %collective-permute-start = (bf16[64,1792]{1,0:T(8,128)(2,1)S(1)}, bf16[64,1792]{1,0:T(8,128)(2,1)}, u32[]{:S(2)}, u32[]{:S(2)}) collective-permute-start(bf16[64,1792]{1,0:T(8,128)(2,1)S(1)} %pad_maximum_fusion.2), channel_id=1, source_target_pairs={{0,64},{1,449},{64,0},{65,129},{128,192},{129,65},{192,128},{193,2... | collective-permute-start | bytes 688136 | tf_op jit(solution)/shard_map/ppermute | solution.py:42
  9.2 3.3 %collective-permute-done = bf16[64,1792]{1,0:T(8,128)(2,1)} collective-permute-done((bf16[64,1792]{1,0:T(8,128)(2,1)S(1)}, bf16[64,1792]{1,0:T(8,128)(2,1)}, u32[]{:S(2)}, u32[]{:S(2)}) %collective-permute-start) | collective-permute-done | bytes 229408 | tf_op jit(solution)/shard_map/ppermute | solution.py:42
  13.3 1.1 bitcast_multiply_fusion
  14.4 7.8 %collective-permute-start.1 = (bf16[512,896]{0,1:T(8,128)(2,1)}, bf16[512,896]{0,1:T(8,128)(2,1)}, u32[]{:S(2)}, u32[]{:S(2)}) collective-permute-start(bf16[512,896]{0,1:T(8,128)(2,1)} %bitcast_multiply_fusion), channel_id=1, source_target_pairs={{0,1},{1,0},{2,3},{3,2},{4,5},{5,4},{6,7},{7,6},{8,9},{9,8},{10,11... | collective-permute-start | bytes 2752520 | tf_op jit(solution)/shard_map/ppermute | solution.py:133
  23.2 4.9 %collective-permute-start.2 = (bf16[128,1792]{1,0:T(8,128)(2,1)S(1)}, bf16[128,1792]{1,0:T(8,128)(2,1)S(1)}, u32[]{:S(2)}, u32[]{:S(2)}) collective-permute-start(bf16[128,1792]{1,0:T(8,128)(2,1)S(1)} %pad_maximum_fusion.1.refs_0_), channel_id=1, source_target_pairs={{0,448},{1,65},{64,128},{65,1},{128,64},{129,193},{192,256},{193,1... | collective-permute-start | bytes 1376264 | tf_op jit(solution)/shard_map/ppermute | solution.py:42
  28.1 3.5 %collective-permute-start.5 = (bf16[64,1792]{1,0:T(8,128)(2,1)S(1)}, bf16[64,1792]{1,0:T(8,128)(2,1)S(1)}, u32[]{:S(2)}, u32[]{:S(2)}) collective-permute-start(bf16[64,1792]{1,0:T(8,128)(2,1)S(1)} %pad_maximum_fusion.2), channel_id=1, source_target_pairs={{0,32},{32,0},{1,33},{33,1},{2,34},{34,2},{3,35},{35,3},{4,36},{36... | collective-permute-start | bytes 688136 | tf_op jit(solution)/shard_map/ppermute | solution.py:126
  32.3 6.2 %all-to-all-start.1 = ((bf16[4,64,512]{2,1,0:T(8,128)(2,1)}), bf16[4,64,512]{2,1,0:T(8,128)(2,1)S(1)}, u32[]{:S(2)}, u32[]{:S(2)}) async-start(bf16[4,64,512]{2,1,0:T(8,128)(2,1)} %broadcast_in_dim.7), calls=%async_computation.1 | async-start | bytes 524288 | tf_op jit(solution)/shard_map/all_to_all | solution.py:47
  38.6 3.3 %collective-permute-start.6 = (bf16[64,1792]{1,0:T(8,128)(2,1)}, bf16[64,1792]{1,0:T(8,128)(2,1)}, u32[]{:S(2)}, u32[]{:S(2)}) collective-permute-start(bf16[64,1792]{1,0:T(8,128)(2,1)} %collective-permute-done), channel_id=1, source_target_pairs={{0,32},{32,0},{1,33},{33,1},{2,34},{34,2},{3,35},{35,3},{4,36},{36... | collective-permute-start | bytes 688136 | tf_op jit(solution)/shard_map/ppermute | solution.py:131
  41.9 2.6 %collective-permute-start.7 = (bf16[128,1792]{1,0:T(8,128)(2,1)S(1)}, bf16[128,1792]{1,0:T(8,128)(2,1)S(1)}, u32[]{:S(2)}, u32[]{:S(2)}) collective-permute-start(bf16[128,1792]{1,0:T(8,128)(2,1)S(1)} %collective-permute-done.2.refs_1_), channel_id=1, source_target_pairs={{0,32},{32,0},{1,33},{33,1},{2,34},{34,2},{3,35},{35,3},{4,36},{36... | collective-permute-start | bytes 1376264 | tf_op jit(solution)/shard_map/ppermute | solution.py:135
  44.5 5.9 %all-to-all-done.1 = bf16[4,64,512]{2,1,0:T(8,128)(2,1)S(1)} async-done(((bf16[4,64,512]{2,1,0:T(8,128)(2,1)}), bf16[4,64,512]{2,1,0:T(8,128)(2,1)S(1)}, u32[]{:S(2)}, u32[]{:S(2)}) %all-to-all-start.1) | async-done | bytes 262176 | tf_op jit(solution)/shard_map/all_to_all | solution.py:47
  50.5 1.1 broadcast_in_dim.8
  51.6 4.8 %all-to-all-start.2 = ((bf16[4,256,512]{2,1,0:T(8,128)(2,1)}), bf16[4,256,512]{2,1,0:T(8,128)(2,1)S(1)}, u32[]{:S(2)}, u32[]{:S(2)}) async-start(bf16[4,256,512]{2,1,0:T(8,128)(2,1)} %broadcast_in_dim.8), calls=%async_computation.2 | async-start | bytes 2097152 | tf_op jit(solution)/shard_map/all_to_all | solution.py:47
  56.4 1.9 %collective-permute-start.3 = (bf16[128,1792]{1,0:T(8,128)(2,1)S(1)}, bf16[128,1792]{1,0:T(8,128)(2,1)S(1)}, u32[]{:S(2)}, u32[]{:S(2)}) collective-permute-start(bf16[128,1792]{1,0:T(8,128)(2,1)S(1)} %collective-permute-done.2.refs_1_), channel_id=1, source_target_pairs={{0,64},{1,449},{64,0},{65,129},{128,192},{129,65},{192,128},{193,2... | collective-permute-start | bytes 1376264 | tf_op jit(solution)/shard_map/ppermute | solution.py:42
  58.3 1.6 %pad_maximum_fusion = bf16[512,1792]{0,1:T(8,128)(2,1)S(1)} fusion(bf16[512,896]{0,1:T(8,128)(2,1)} %collective-permute-done.1, bf16[512,896]{0,1:T(8,128)(2,1)} %bitcast_multiply_fusion), kind=kLoop, calls=%fused_computation | loop fusion | flops 3670016 | bytes 3670016 | tf_op jit(solution)/shard_map/concatenate | solution.py:133
  59.9 3.9 %collective-permute-start.8 = (bf16[128,1792]{1,0:T(8,128)(2,1)S(1)}, bf16[128,1792]{1,0:T(8,128)(2,1)S(1)}, u32[]{:S(2)}, u32[]{:S(2)}) collective-permute-start(bf16[128,1792]{1,0:T(8,128)(2,1)S(1)} %collective-permute-done.7.refs_5_), channel_id=1, source_target_pairs={{0,64},{1,449},{64,0},{65,129},{128,192},{129,65},{192,128},{193,2... | collective-permute-start | bytes 1376264 | tf_op jit(solution)/shard_map/ppermute | solution.py:42
  64.2 2.5 %collective-permute-done.3.refs_2_ = bf16[128,1792]{1,0:T(8,128)(2,1)S(1)} collective-permute-done((bf16[128,1792]{1,0:T(8,128)(2,1)S(1)}, bf16[128,1792]{1,0:T(8,128)(2,1)S(1)}, u32[]{:S(2)}, u32[]{:S(2)}) %collective-permute-start.3) | collective-permute-done | bytes 458784 | tf_op jit(solution)/shard_map/ppermute | solution.py:42
  67.1 2.2 %collective-permute-start.4 = (bf16[128,1792]{1,0:T(8,128)(2,1)S(1)}, bf16[128,1792]{1,0:T(8,128)(2,1)S(1)}, u32[]{:S(2)}, u32[]{:S(2)}) collective-permute-start(bf16[128,1792]{1,0:T(8,128)(2,1)S(1)} %collective-permute-done.3.refs_2_), channel_id=1, source_target_pairs={{0,448},{1,65},{64,128},{65,1},{128,64},{129,193},{192,256},{193,1... | collective-permute-start | bytes 1376264 | tf_op jit(solution)/shard_map/ppermute | solution.py:42
  69.7 1.3 %convolution_convert_fusion.7.refs_0_ = bf16[128,512]{1,0:T(8,128)(2,1)S(1)} fusion(bf16[512,1792]{0,1:T(8,128)(2,1)S(1)} %pad_maximum_fusion, bf16[64,1792]{1,0:T(8,128)(2,1)} %collective-permute-done, bf16[64,896]{1,0:T(8,128)(2,1)S(1)} %copy-done.10, bf16[64,896]{1,0:T(8,128)(2,1)S(1)} %constant_dynamic-slice_fusion), kind=kOutput, calls=%fused_computation.8 | convolution fusion | flops 236322816 | bytes 2424832 | tf_op jit(solution)/shard_map/dot_general | solution.py:24
  71.1 4.7 %collective-permute-done.8.refs_6_ = bf16[128,1792]{1,0:T(8,128)(2,1)S(1)} collective-permute-done((bf16[128,1792]{1,0:T(8,128)(2,1)S(1)}, bf16[128,1792]{1,0:T(8,128)(2,1)S(1)}, u32[]{:S(2)}, u32[]{:S(2)}) %collective-permute-start.8) | collective-permute-done | bytes 458784 | tf_op jit(solution)/shard_map/ppermute | solution.py:42
  75.8 1.1 constant_dynamic-update-slice_fusion.refs_4_
  76.9 1.9 %collective-permute-start.9 = (bf16[128,1792]{1,0:T(8,128)(2,1)S(1)}, bf16[128,1792]{1,0:T(8,128)(2,1)S(1)}, u32[]{:S(2)}, u32[]{:S(2)}) collective-permute-start(bf16[128,1792]{1,0:T(8,128)(2,1)S(1)} %collective-permute-done.8.refs_6_), channel_id=1, source_target_pairs={{0,448},{1,65},{64,128},{65,1},{128,64},{129,193},{192,256},{193,1... | collective-permute-start | bytes 1376264 | tf_op jit(solution)/shard_map/ppermute | solution.py:42
  80.1 8.4 %collective-permute-done.9.refs_7_ = bf16[128,1792]{1,0:T(8,128)(2,1)S(1)} collective-permute-done((bf16[128,1792]{1,0:T(8,128)(2,1)S(1)}, bf16[128,1792]{1,0:T(8,128)(2,1)S(1)}, u32[]{:S(2)}, u32[]{:S(2)}) %collective-permute-start.9) | collective-permute-done | bytes 458784 | tf_op jit(solution)/shard_map/ppermute | solution.py:42
  89.7 1.6 %shard_map.59 = bf16[1024,512]{1,0:T(8,128)(2,1)} custom-call(s32[16]{0:T(128)S(1)} %stack.67.order, bf16[128,512]{1,0:T(8,128)(2,1)S(1)} %convolution_convert_fusion.7.refs_0_, bf16[128,512]{1,0:T(8,128)(2,1)S(1)} %convolution_convert_fusion.6.refs_1_, bf16[128,512]{1,0:T(8,128)(2,1)S(1)} %convolution_convert_fusion.5.refs_2_, ...), custom_call_target="tpu_custom_call" | custom-call | tf_op jit(solution)/shard_map/pallas_call | solution.py:56
  91.3 5.5 %all-to-all-start = ((bf16[16,64,512]{2,1,0:T(8,128)(2,1)}), bf16[16,64,512]{2,1,0:T(8,128)(2,1)}, u32[]{:S(2)}, u32[]{:S(2)}) async-start(bf16[16,64,512]{2,1,0:T(8,128)(2,1)} %bitcast.18), calls=%async_computation | async-start | bytes 2097152 | tf_op jit(solution)/shard_map/all_to_all | solution.py:145
  97.8 1.0 copy-done.4
  99.8 1.9 %shard_map.60 = (bf16[1024,512]{1,0:T(8,128)(2,1)S(1)}, bf16[512,896]{1,0:T(8,128)(2,1)S(1)}) custom-call(s32[16]{0:T(128)S(1)} %stack.67.order, bf16[16,64,512]{2,1,0:T(8,128)(2,1)S(1)} %bitcast.43, bf16[128,1792]{1,0:T(8,128)(2,1)S(1)} %pad_maximum_fusion.1.refs_0_, bf16[128,1792]{1,0:T(8,128)(2,1)S(1)} %collective-permute-done.2.refs_1_, ...), custom_call_target="tpu_custom_call" | custom-call | tf_op jit(solution)/shard_map/pallas_call | solution.py:56
  101.7 1.9 %collective-permute-start.10 = (bf16[512,896]{1,0:T(8,128)(2,1)S(1)}, bf16[512,896]{1,0:T(8,128)(2,1)S(1)}, u32[]{:S(2)}, u32[]{:S(2)}) collective-permute-start(bf16[512,896]{1,0:T(8,128)(2,1)S(1)} %get-tuple-element.16), channel_id=1, source_target_pairs={{0,1},{1,0},{2,3},{3,2},{4,5},{5,4},{6,7},{7,6},{8,9},{9,8},{10,11... | collective-permute-start | bytes 2752520 | tf_op jit(solution)/shard_map/ppermute | solution.py:148
  103.6 2.4 %collective-permute-done.10.received = bf16[512,896]{1,0:T(8,128)(2,1)S(1)} collective-permute-done((bf16[512,896]{1,0:T(8,128)(2,1)S(1)}, bf16[512,896]{1,0:T(8,128)(2,1)S(1)}, u32[]{:S(2)}, u32[]{:S(2)}) %collective-permute-start.10) | collective-permute-done | bytes 917536 | tf_op jit(solution)/shard_map/ppermute | solution.py:148
  106.1 2.8 %shard_map.61 = bf16[512,896]{1,0:T(8,128)(2,1)} custom-call(s32[4,7]{1,0:T(4,128)S(1)} %copy-done.8, bf16[1024,512]{1,0:T(8,128)(2,1)S(1)} %get-tuple-element.15.in_rows, bf16[512,896]{1,0:T(8,128)(2,1)S(1)} %collective-permute-done.10.received, bf16[128,1792]{1,0:T(8,128)(2,1)S(1)} %pad_maximum_fusion.1.refs_0_, ...), custom_call_target="tpu_custom_call" | custom-call | tf_op jit(solution)/shard_map/pallas_call | solution.py:56
  108.9 9.6 %all-to-all-done = bf16[16,64,512]{2,1,0:T(8,128)(2,1)} async-done(((bf16[16,64,512]{2,1,0:T(8,128)(2,1)}), bf16[16,64,512]{2,1,0:T(8,128)(2,1)}, u32[]{:S(2)}, u32[]{:S(2)}) %all-to-all-start) | async-done | bytes 1048608 | tf_op jit(solution)/shard_map/all_to_all | solution.py:145
  118.5 2.0 %reduce_sum.12 = bf16[64,512]{1,0:T(8,128)(2,1)} reduce(bf16[16,64,512]{2,1,0:T(8,128)(2,1)} %all-to-all-done, bf16[]{:T(256)} %constant.231.clone.1), dimensions={0}, to_apply=%region_0.1 | reduce | flops 491520 | bytes 1114114 | tf_op jit(solution)/shard_map/reduce_sum | solution.py:152
  (50 shorter events, 10.1 us)
Async XLA Ops:
  0.6 11.9 %copy-start.11 = (bf16[512,896]{1,0:T(8,128)(2,1)S(1)}, bf16[512,896]{1,0:T(8,128)(2,1)}, u32[]{:S(2)}) copy-start(bf16[512,896]{1,0:T(8,128)(2,1)} %param.6) | copy-start | bytes 2752516
  4.1 18.2 %copy-start.9 = (bf16[64,896]{1,0:T(8,128)(2,1)}, bf16[64,896]{1,0:T(8,128)(2,1)S(1)}, u32[]{:S(2)}) copy-start(bf16[64,896]{1,0:T(8,128)(2,1)S(1)} %dynamic-slice_bitcast_fusion) | copy-start | bytes 344068
  4.1 8.4 %collective-permute-start = (bf16[64,1792]{1,0:T(8,128)(2,1)S(1)}, bf16[64,1792]{1,0:T(8,128)(2,1)}, u32[]{:S(2)}, u32[]{:S(2)}) collective-permute-start(bf16[64,1792]{1,0:T(8,128)(2,1)S(1)} %pad_maximum_fusion.2), channel_id=1, source_target_pairs={{0,64},{1,449},{64,0},{65,129},{128,192},{129,65},{192,128},{193,2... | collective-permute-start | bytes 688136 | tf_op jit(solution)/shard_map/ppermute | solution.py:42
  13.3 18.3 %copy-start.12 = (bf16[64,512]{1,0:T(8,128)(2,1)S(1)}, bf16[64,512]{1,0:T(8,128)(2,1)}, u32[]{:S(2)}) copy-start(bf16[64,512]{1,0:T(8,128)(2,1)} %param.4) | copy-start | bytes 196612
  14.4 43.9 %collective-permute-start.1 = (bf16[512,896]{0,1:T(8,128)(2,1)}, bf16[512,896]{0,1:T(8,128)(2,1)}, u32[]{:S(2)}, u32[]{:S(2)}) collective-permute-start(bf16[512,896]{0,1:T(8,128)(2,1)} %bitcast_multiply_fusion), channel_id=1, source_target_pairs={{0,1},{1,0},{2,3},{3,2},{4,5},{5,4},{6,7},{7,6},{8,9},{9,8},{10,11... | collective-permute-start | bytes 2752520 | tf_op jit(solution)/shard_map/ppermute | solution.py:133
  23.2 18.7 %collective-permute-start.2 = (bf16[128,1792]{1,0:T(8,128)(2,1)S(1)}, bf16[128,1792]{1,0:T(8,128)(2,1)S(1)}, u32[]{:S(2)}, u32[]{:S(2)}) collective-permute-start(bf16[128,1792]{1,0:T(8,128)(2,1)S(1)} %pad_maximum_fusion.1.refs_0_), channel_id=1, source_target_pairs={{0,448},{1,65},{64,128},{65,1},{128,64},{129,193},{192,256},{193,1... | collective-permute-start | bytes 1376264 | tf_op jit(solution)/shard_map/ppermute | solution.py:42
  28.1 16.4 %collective-permute-start.5 = (bf16[64,1792]{1,0:T(8,128)(2,1)S(1)}, bf16[64,1792]{1,0:T(8,128)(2,1)S(1)}, u32[]{:S(2)}, u32[]{:S(2)}) collective-permute-start(bf16[64,1792]{1,0:T(8,128)(2,1)S(1)} %pad_maximum_fusion.2), channel_id=1, source_target_pairs={{0,32},{32,0},{1,33},{33,1},{2,34},{34,2},{3,35},{35,3},{4,36},{36... | collective-permute-start | bytes 688136 | tf_op jit(solution)/shard_map/ppermute | solution.py:126
  32.3 18.1 %all-to-all-start.1 = ((bf16[4,64,512]{2,1,0:T(8,128)(2,1)}), bf16[4,64,512]{2,1,0:T(8,128)(2,1)S(1)}, u32[]{:S(2)}, u32[]{:S(2)}) async-start(bf16[4,64,512]{2,1,0:T(8,128)(2,1)} %broadcast_in_dim.7), calls=%async_computation.1 | async-start | bytes 524288 | tf_op jit(solution)/shard_map/all_to_all | solution.py:47
  38.6 32.5 %collective-permute-start.6 = (bf16[64,1792]{1,0:T(8,128)(2,1)}, bf16[64,1792]{1,0:T(8,128)(2,1)}, u32[]{:S(2)}, u32[]{:S(2)}) collective-permute-start(bf16[64,1792]{1,0:T(8,128)(2,1)} %collective-permute-done), channel_id=1, source_target_pairs={{0,32},{32,0},{1,33},{33,1},{2,34},{34,2},{3,35},{35,3},{4,36},{36... | collective-permute-start | bytes 688136 | tf_op jit(solution)/shard_map/ppermute | solution.py:131
  41.9 18.0 %collective-permute-start.7 = (bf16[128,1792]{1,0:T(8,128)(2,1)S(1)}, bf16[128,1792]{1,0:T(8,128)(2,1)S(1)}, u32[]{:S(2)}, u32[]{:S(2)}) collective-permute-start(bf16[128,1792]{1,0:T(8,128)(2,1)S(1)} %collective-permute-done.2.refs_1_), channel_id=1, source_target_pairs={{0,32},{32,0},{1,33},{33,1},{2,34},{34,2},{3,35},{35,3},{4,36},{36... | collective-permute-start | bytes 1376264 | tf_op jit(solution)/shard_map/ppermute | solution.py:135
  51.6 39.7 %all-to-all-start.2 = ((bf16[4,256,512]{2,1,0:T(8,128)(2,1)}), bf16[4,256,512]{2,1,0:T(8,128)(2,1)S(1)}, u32[]{:S(2)}, u32[]{:S(2)}) async-start(bf16[4,256,512]{2,1,0:T(8,128)(2,1)} %broadcast_in_dim.8), calls=%async_computation.2 | async-start | bytes 2097152 | tf_op jit(solution)/shard_map/all_to_all | solution.py:47
  56.4 10.4 %collective-permute-start.3 = (bf16[128,1792]{1,0:T(8,128)(2,1)S(1)}, bf16[128,1792]{1,0:T(8,128)(2,1)S(1)}, u32[]{:S(2)}, u32[]{:S(2)}) collective-permute-start(bf16[128,1792]{1,0:T(8,128)(2,1)S(1)} %collective-permute-done.2.refs_1_), channel_id=1, source_target_pairs={{0,64},{1,449},{64,0},{65,129},{128,192},{129,65},{192,128},{193,2... | collective-permute-start | bytes 1376264 | tf_op jit(solution)/shard_map/ppermute | solution.py:42
  59.9 15.9 %collective-permute-start.8 = (bf16[128,1792]{1,0:T(8,128)(2,1)S(1)}, bf16[128,1792]{1,0:T(8,128)(2,1)S(1)}, u32[]{:S(2)}, u32[]{:S(2)}) collective-permute-start(bf16[128,1792]{1,0:T(8,128)(2,1)S(1)} %collective-permute-done.7.refs_5_), channel_id=1, source_target_pairs={{0,64},{1,449},{64,0},{65,129},{128,192},{129,65},{192,128},{193,2... | collective-permute-start | bytes 1376264 | tf_op jit(solution)/shard_map/ppermute | solution.py:42
  64.2 5.5 %copy-start.10 = (bf16[64,896]{1,0:T(8,128)(2,1)S(1)}, bf16[64,896]{1,0:T(8,128)(2,1)}, u32[]{:S(2)}) copy-start(bf16[64,896]{1,0:T(8,128)(2,1)} %copy-done.9) | copy-start | bytes 344068
  67.1 12.5 %collective-permute-start.4 = (bf16[128,1792]{1,0:T(8,128)(2,1)S(1)}, bf16[128,1792]{1,0:T(8,128)(2,1)S(1)}, u32[]{:S(2)}, u32[]{:S(2)}) collective-permute-start(bf16[128,1792]{1,0:T(8,128)(2,1)S(1)} %collective-permute-done.3.refs_2_), channel_id=1, source_target_pairs={{0,448},{1,65},{64,128},{65,1},{128,64},{129,193},{192,256},{193,1... | collective-permute-start | bytes 1376264 | tf_op jit(solution)/shard_map/ppermute | solution.py:42
  75.8 3.9 %copy-start = (bf16[128,1792]{1,0:T(8,128)(2,1)}, bf16[128,1792]{1,0:T(8,128)(2,1)S(1)}, u32[]{:S(2)}) copy-start(bf16[128,1792]{1,0:T(8,128)(2,1)S(1)} %collective-permute-done.8.refs_6_) | copy-start | bytes 1376260
  76.9 11.6 %collective-permute-start.9 = (bf16[128,1792]{1,0:T(8,128)(2,1)S(1)}, bf16[128,1792]{1,0:T(8,128)(2,1)S(1)}, u32[]{:S(2)}, u32[]{:S(2)}) collective-permute-start(bf16[128,1792]{1,0:T(8,128)(2,1)S(1)} %collective-permute-done.8.refs_6_), channel_id=1, source_target_pairs={{0,448},{1,65},{64,128},{65,1},{128,64},{129,193},{192,256},{193,1... | collective-permute-start | bytes 1376264 | tf_op jit(solution)/shard_map/ppermute | solution.py:42
  79.7 8.8 %copy-start.3 = (bf16[128,1792]{1,0:T(8,128)(2,1)}, bf16[128,1792]{1,0:T(8,128)(2,1)S(1)}, u32[]{:S(2)}) copy-start(bf16[128,1792]{1,0:T(8,128)(2,1)S(1)} %collective-permute-done.4.refs_3_) | copy-start | bytes 1376260
  88.9 0.8 copy-start.5
  91.3 27.3 %all-to-all-start = ((bf16[16,64,512]{2,1,0:T(8,128)(2,1)}), bf16[16,64,512]{2,1,0:T(8,128)(2,1)}, u32[]{:S(2)}, u32[]{:S(2)}) async-start(bf16[16,64,512]{2,1,0:T(8,128)(2,1)} %bitcast.18), calls=%async_computation | async-start | bytes 2097152 | tf_op jit(solution)/shard_map/all_to_all | solution.py:145
  96.7 1.0 copy-start.1
  97.8 1.0 copy-start.4
  98.8 1.0 copy-start.6
  99.8 6.2 %copy-start.2 = (bf16[128,1792]{1,0:T(8,128)(2,1)S(1)}, bf16[128,1792]{1,0:T(8,128)(2,1)}, u32[]{:S(2)}) copy-start(bf16[128,1792]{1,0:T(8,128)(2,1)} %copy-done) | copy-start | bytes 1376260
  99.8 6.2 %copy-start.7 = (bf16[128,1792]{1,0:T(8,128)(2,1)S(1)}, bf16[128,1792]{1,0:T(8,128)(2,1)}, u32[]{:S(2)}) copy-start(bf16[128,1792]{1,0:T(8,128)(2,1)} %copy-done.5) | copy-start | bytes 1376260
  99.8 6.2 %copy-start.8 = (s32[4,7]{1,0:T(4,128)S(1)}, s32[4,7]{1,0:T(4,128)}, u32[]{:S(2)}) copy-start(s32[4,7]{1,0:T(4,128)} %mask.1) | copy-start | bytes 340
  101.7 4.4 %collective-permute-start.10 = (bf16[512,896]{1,0:T(8,128)(2,1)S(1)}, bf16[512,896]{1,0:T(8,128)(2,1)S(1)}, u32[]{:S(2)}, u32[]{:S(2)}) collective-permute-start(bf16[512,896]{1,0:T(8,128)(2,1)S(1)} %get-tuple-element.16), channel_id=1, source_target_pairs={{0,1},{1,0},{2,3},{3,2},{4,5},{5,4},{6,7},{7,6},{8,9},{9,8},{10,11... | collective-permute-start | bytes 2752520 | tf_op jit(solution)/shard_map/ppermute | solution.py:148
